TPU v7x, 1024 devices: a whole 8x8x8 slice. The times are simulated.
1024 devices in a mesh: dp: 2 (over core), expert: 64 (over y, z), tensor: 8 (over x).
Axes of the slice: x: 8, y: 8, z: 8, core: 2. Of those that a mesh axis runs over, the one named last changes fastest.
Arguments:
- grad_out: bfloat16 [4096, 3584], P(('dp', 'expert', 'tensor')), parts along dimension 0, may hold values from -6 to 6
- routes: int32 [4096, 2], P(('dp', 'expert')), parts along dimension 0, may hold values from 0 to 63, all different within a row; in each aligned block of 32 rows (0 to 31, 32 to 63, ...) at most 2 rows name the same one
- gate_probs: bfloat16 [4096, 2], P(('dp', 'expert')), parts along dimension 0, may hold values from 0.099609375 to 0.8984375
- dense_gate_pre: bfloat16 [4096, 2432], P(('dp', 'expert'), 'tensor'), parts along dimension 0, may hold values from -6 to 6
- dense_up_pre: bfloat16 [4096, 2432], P(('dp', 'expert'), 'tensor'), parts along dimension 0, may hold values from -6 to 6
- dense_w_gate: bfloat16 [3584, 2432], P('expert', 'tensor'), may hold values from -0.125 to 0.125
- dense_w_up: bfloat16 [3584, 2432], P('expert', 'tensor'), may hold values from -0.125 to 0.125
- dense_w_down: bfloat16 [2432, 3584], P('tensor'), may hold values from -0.09375 to 0.09375
- expert_gate_pre: bfloat16 [128, 128, 2432], P(('dp', 'expert'), None, 'tensor'), parts along dimension 0, may hold values from -6 to 6
- expert_up_pre: bfloat16 [128, 128, 2432], P(('dp', 'expert'), None, 'tensor'), parts along dimension 0, may hold values from -6 to 6
- expert_w_gate: bfloat16 [64, 3584, 2432], P('expert', None, 'tensor'), may hold values from -0.125 to 0.125
- expert_w_up: bfloat16 [64, 3584, 2432], P('expert', None, 'tensor'), may hold values from -0.125 to 0.125
- expert_w_down: bfloat16 [64, 2432, 3584], P('expert', 'tensor'), may hold values from -0.09375 to 0.09375
Outputs:
- grad_in: bfloat16 [4096, 3584], P(('dp', 'expert', 'tensor')), parts along dimension 0
There are 2 independent parts, one for each index of `dp`. A program takes and returns all parts, laid end to end along the dimension named above; an argument that names none is the same for every part. Nothing has to cross between parts.
Inputs may be any that keep to these rules, and one draw needn't show every extreme that they name: `routes`: each token names two different experts. Within each token group of 32 tokens no expert is named by more than 2 tokens, a bound that some block reaches.
All inputs are finite; a program needn't handle non-finite values.
Results may differ from a plain program's by a relative error of at most 0.017.
Values may be sent and summed in bfloat16 or wider, within the bound.
A program may use at most 64 MiB of HBM per device.

v0:
```python
import jax
import jax.numpy as jnp
from jax import lax
from jax.sharding import PartitionSpec as P


def swiglu_back(upstream, gate_pre, up_pre):
    gate_value = gate_pre.astype(jnp.float32)
    up_value = up_pre.astype(jnp.float32)
    sigmoid_gate = jax.nn.sigmoid(gate_value)
    silu_value = gate_value * sigmoid_gate
    silu_slope = sigmoid_gate * (1.0 + gate_value * (1.0 - sigmoid_gate))
    grad_gate = (upstream * up_value * silu_slope).astype(jnp.bfloat16)
    grad_up = (upstream * silu_value).astype(jnp.bfloat16)
    return (grad_gate, grad_up)


def slot_targets(routes, capacity, experts):
    pair_expert = routes.reshape(-1)
    expert_ids = jnp.arange(experts, dtype=jnp.int32)
    expert_hits = (pair_expert[:, None] == expert_ids[None, :]).astype(jnp.int32)
    earlier = jnp.cumsum(expert_hits, axis=0) - expert_hits
    slot_index = jnp.sum(earlier * expert_hits, axis=1)
    return pair_expert * capacity + slot_index


def token_table(targets, weights, columns_count):
    columns = jnp.arange(columns_count, dtype=jnp.int32)
    marks = (targets.reshape(-1, 2)[:, :, None] == columns[None, None, :]).astype(jnp.float32)
    return jnp.sum(marks * weights.astype(jnp.float32)[:, :, None], axis=1).astype(jnp.bfloat16)


def dense_branch(group_grad, dense_gate_pre, dense_up_pre, dense_w_gate, dense_w_up, dense_w_down):
    upstream = jnp.einsum("td,fd->tf", group_grad, dense_w_down, preferred_element_type=jnp.float32)
    grad_gate, grad_up = swiglu_back(upstream, dense_gate_pre, dense_up_pre)
    block = jnp.einsum(
        "tf,rf->tr",
        grad_gate,
        lax.all_gather(dense_w_gate, "expert", axis=0, tiled=True),
        preferred_element_type=jnp.float32,
    )
    return block + jnp.einsum(
        "tf,rf->tr",
        grad_up,
        lax.all_gather(dense_w_up, "expert", axis=0, tiled=True),
        preferred_element_type=jnp.float32,
    )


def send_routed(group_grad, targets, experts, capacity, w_down):
    width = group_grad.shape[1]
    ones_weights = jnp.ones((group_grad.shape[0], 2), jnp.float32)
    table_ones = token_table(targets, ones_weights, experts * capacity)
    outgoing = jnp.einsum("tc,td->cd", table_ones, group_grad, preferred_element_type=jnp.float32)
    outgoing = outgoing.astype(jnp.bfloat16).reshape(experts, capacity, width)
    received = lax.all_to_all(outgoing, "expert", split_axis=0, concat_axis=0, tiled=True)
    slot_rows = received.reshape(-1, width)
    upstream = jnp.einsum("sd,fd->sf", slot_rows, w_down, preferred_element_type=jnp.float32)
    return upstream


def body(
    grad_out,
    routes,
    gate_probs,
    dense_gate_pre,
    dense_up_pre,
    dense_w_gate,
    dense_w_up,
    dense_w_down,
    expert_gate_pre,
    expert_up_pre,
    expert_w_gate,
    expert_w_up,
    expert_w_down,
):
    experts = lax.axis_size("expert")
    width = grad_out.shape[1]
    capacity = expert_gate_pre.shape[1] // experts
    group_grad = lax.all_gather(grad_out, "tensor", axis=0, tiled=True)
    targets = slot_targets(routes, capacity, experts)
    dense_part = dense_branch(
        group_grad, dense_gate_pre, dense_up_pre, dense_w_gate, dense_w_up, dense_w_down
    )
    upstream = send_routed(group_grad, targets, experts, capacity, expert_w_down[0])
    expert_gg, expert_gu = swiglu_back(upstream, expert_gate_pre[0], expert_up_pre[0])
    backward = jnp.einsum(
        "sf,df->sd", expert_gg, expert_w_gate[0], preferred_element_type=jnp.float32
    )
    backward = backward + jnp.einsum(
        "sf,df->sd", expert_gu, expert_w_up[0], preferred_element_type=jnp.float32
    )
    backward = backward.astype(jnp.bfloat16).reshape(experts, capacity, width)
    returned = lax.all_to_all(backward, "expert", split_axis=0, concat_axis=0, tiled=True)
    weighted = token_table(targets, gate_probs, experts * capacity)
    routed_part = jnp.einsum(
        "tc,cd->td", weighted, returned.reshape(-1, width), preferred_element_type=jnp.float32
    )
    summed = lax.psum_scatter(
        (dense_part + routed_part).astype(jnp.bfloat16), "tensor", scatter_dimension=0, tiled=True
    ).astype(jnp.float32)
    return (grad_out.astype(jnp.float32) + summed).astype(jnp.bfloat16)


def solution(mesh):
    return jax.shard_map(
        body,
        mesh=mesh,
        in_specs=(
            P(("dp", "expert", "tensor"), None),
            P(("dp", "expert"), None),
            P(("dp", "expert"), None),
            P(("dp", "expert"), "tensor"),
            P(("dp", "expert"), "tensor"),
            P("expert", "tensor"),
            P("expert", "tensor"),
            P("tensor", None),
            P(("dp", "expert"), None, "tensor"),
            P(("dp", "expert"), None, "tensor"),
            P("expert", None, "tensor"),
            P("expert", None, "tensor"),
            P("expert", "tensor", None),
        ),
        out_specs=P(("dp", "expert", "tensor"), None),
        check_vma=False,
    )
```

profile of v0, /device:TPU:14, one launch (start us, length us, event | category | flops | bytes accessed | tf_op | source)
XLA Modules:
  0.0 325.2 jit_solution(14626252868511737211)
XLA Ops:
  6.5 0.0 copy-start
  6.5 0.0 all-gather.4.cloned.1.call-start
  6.5 0.7 all-gather.4.cloned.1.call-update
  7.3 34.8 %all-gather = bf16[8,4,3584]{2,1,0:T(4,128)(2,1)S(1)} all-gather(bf16[1,4,3584]{2,1,0:T(4,128)(2,1)} %bitcast.36), channel_id=1, replica_groups=mesh['dp'=2,'expert'=64,'tensor'=8] {'tensor'}, dimensions={0}, use_global_device_ids=true | all-gather | bytes 258048 | tf_op jit(solution)/shard_map/all_gather | solution.py:80
  42.1 0.1 reshape.32
  42.1 0.7 convert_element_type.70
  42.8 0.8 copy.30
  43.5 0.1 eq.14
  43.7 0.1 fusion.32
  43.7 0.1 reduce_window_sum.11
  43.8 0.2 select_reduce_fusion.1
  44.0 0.1 reduce_sum.30
  44.1 0.1 copy.31
  44.2 0.7 multiply_add_fusion
  44.9 0.7 select_reduce_fusion
  45.6 0.4 convolution_convert_fusion
  46.0 1.3 reshape.25
  47.3 13.6 %all-to-all-start = ((bf16[64,2,3584]{2,1,0:T(2,128)(2,1)}), bf16[64,2,3584]{2,1,0:T(2,128)(2,1)S(1)}, u32[]{:S(2)}, u32[]{:S(2)}) async-start(bf16[64,2,3584]{2,1,0:T(2,128)(2,1)} %reshape.25), calls=%async_computation | async-start | bytes 1835008 | tf_op jit(solution)/shard_map/all_to_all | solution.py:56
  61.0 0.0 all-gather.6.cloned.1.call-start
  61.0 0.7 all-gather.6.cloned.1.call-update
  61.7 0.0 copy-start.2
  61.7 0.0 copy-start.3
  61.7 20.5 %all-to-all-done = bf16[64,2,3584]{2,1,0:T(2,128)(2,1)S(1)} async-done(((bf16[64,2,3584]{2,1,0:T(2,128)(2,1)}), bf16[64,2,3584]{2,1,0:T(2,128)(2,1)S(1)}, u32[]{:S(2)}, u32[]{:S(2)}) %all-to-all-start) | async-done | bytes 917536 | tf_op jit(solution)/shard_map/all_to_all | solution.py:56
  82.2 1.3 reshape.26
  83.5 2.6 fusion.5
  86.1 0.0 copy-done
  86.1 0.0 copy-done.2
  86.1 0.0 copy-done.3
  86.2 0.0 copy-start.1
  86.2 0.7 fusion.3
  86.9 0.9 copy-done.1
  87.8 0.7 fusion
  88.5 1.3 reshape.27
  89.8 6.9 %all-to-all-start.1 = ((bf16[64,2,3584]{2,1,0:T(2,128)(2,1)}), bf16[64,2,3584]{2,1,0:T(2,128)(2,1)}, u32[]{:S(2)}, u32[]{:S(2)}) async-start(bf16[64,2,3584]{2,1,0:T(2,128)(2,1)} %reshape.27), calls=%async_computation.1 | async-start | bytes 1835008 | tf_op jit(solution)/shard_map/all_to_all | solution.py:94
  96.7 0.0 all-reduce.3.cloned.1.call-start
  96.7 3.0 fusion.44
  99.7 23.4 %all-to-all-done.1 = bf16[64,2,3584]{2,1,0:T(2,128)(2,1)} async-done(((bf16[64,2,3584]{2,1,0:T(2,128)(2,1)}), bf16[64,2,3584]{2,1,0:T(2,128)(2,1)}, u32[]{:S(2)}, u32[]{:S(2)}) %all-to-all-start.1) | async-done | bytes 917536 | tf_op jit(solution)/shard_map/all_to_all | solution.py:94
  123.1 2.5 reshape.28
  125.6 13.6 %all-gather.4.cloned.1.call-done = bf16[3584,304]{1,0:T(8,128)(2,1)} async-done(((bf16[56,304]{1,0:T(8,128)(2,1)}), bf16[3584,304]{1,0:T(8,128)(2,1)}) %all-gather.4.cloned.1.call-update) | async-done | bytes 2179088 | tf_op jit(solution)/shard_map/all_gather | solution.py:39
  139.2 2.8 fusion.34
  142.0 91.9 %all-gather.6.cloned.1.call-done = bf16[3584,304]{1,0:T(8,128)(2,1)} async-done(((bf16[56,304]{1,0:T(8,128)(2,1)}), bf16[3584,304]{1,0:T(8,128)(2,1)}) %all-gather.6.cloned.1.call-update) | async-done | bytes 2179088 | tf_op jit(solution)/shard_map/all_gather | solution.py:45
  233.9 0.0 copy-start.4
  233.9 2.8 convolution_add_fusion.2
  236.6 0.0 copy-done.4
  236.7 1.0 fusion.1
  237.6 0.0 all-reduce.3.cloned.1.call-update
  237.6 1.3 dynamic-slice
  239.6 77.6 %all-reduce.3.cloned.1.call-done = bf16[32,3584]{1,0:T(8,128)(2,1)} async-done(((bf16[32,3584]{1,0:T(8,128)(2,1)}), bf16[32,3584]{1,0:T(8,128)(2,1)}) %all-reduce.3.cloned.1.call-update) | async-done | bytes 229392
  317.2 1.5 add_convert_fusion
Async XLA Ops:
  6.5 79.6 %copy-start = (bf16[1,3584,304]{1,2,0:T(8,128)(2,1)S(1)}, bf16[1,3584,304]{1,2,0:T(8,128)(2,1)}, u32[]{:S(2)}) copy-start(bf16[1,3584,304]{1,2,0:T(8,128)(2,1)} %param.23) | copy-start | bytes 6537220
  6.5 132.7 %all-gather.4.cloned.1.call-start = ((), (), s32[]{:S(2)}) async-start(), calls=%async_computation.2 | async-start | bytes 2795520 | tf_op jit(solution)/shard_map/all_gather | solution.py:39
  47.3 34.9 %all-to-all-start = ((bf16[64,2,3584]{2,1,0:T(2,128)(2,1)}), bf16[64,2,3584]{2,1,0:T(2,128)(2,1)S(1)}, u32[]{:S(2)}, u32[]{:S(2)}) async-start(bf16[64,2,3584]{2,1,0:T(2,128)(2,1)} %reshape.25), calls=%async_computation | async-start | bytes 1835008 | tf_op jit(solution)/shard_map/all_to_all | solution.py:56
  61.0 172.9 %all-gather.6.cloned.1.call-start = ((), (), s32[]{:S(2)}) async-start(), calls=%async_computation.3 | async-start | bytes 2795520 | tf_op jit(solution)/shard_map/all_gather | solution.py:45
  61.7 24.4 %copy-start.2 = (bf16[1,128,304]{1,2,0:T(8,128)(2,1)S(1)}, bf16[1,128,304]{1,2,0:T(8,128)(2,1)}, u32[]{:S(2)}) copy-start(bf16[1,128,304]{1,2,0:T(8,128)(2,1)} %param.21) | copy-start | bytes 233476
  61.7 24.4 %copy-start.3 = (bf16[1,128,304]{1,2,0:T(8,128)(2,1)S(1)}, bf16[1,128,304]{1,2,0:T(8,128)(2,1)}, u32[]{:S(2)}) copy-start(bf16[1,128,304]{1,2,0:T(8,128)(2,1)} %param.22) | copy-start | bytes 233476
  86.2 1.6 copy-start.1
  89.8 33.3 %all-to-all-start.1 = ((bf16[64,2,3584]{2,1,0:T(2,128)(2,1)}), bf16[64,2,3584]{2,1,0:T(2,128)(2,1)}, u32[]{:S(2)}, u32[]{:S(2)}) async-start(bf16[64,2,3584]{2,1,0:T(2,128)(2,1)} %reshape.27), calls=%async_computation.1 | async-start | bytes 1835008 | tf_op jit(solution)/shard_map/all_to_all | solution.py:94
  96.7 220.5 %all-reduce.3.cloned.1.call-start = ((), (), s32[]{:S(2)}) async-start(), calls=%async_computation.4 | async-start | bytes 458752
  233.9 2.8 copy-start.4
Sparse Core Ops, SparseCore 0:
  11.6 127.5 all-gather.3
  143.4 90.3 all-gather.5
  237.8 79.3 all-reduce.2
where the time goes:
time: 326 us; the launch traced here: 325 us
  waiting for transfers between devices  228 us (70%)
  blocking collectives  34.8 us (11%)
  starting transfers between devices  20.6 us (6%)
  matrix products  13.9 us (4%)
  between operations  13.9 us (4%)
  local copies, waits for them, and re-layouts  9.65 us (3%)
  other arithmetic  3.87 us (1%)
    all_gather x1, waiting for transfers between devices, dense_branch(): lax.all_gather(dense_w_up, 'expert', axis=0, tiled=True)  91.9 us
    unnamed x4, waiting for transfers between devices  79 us
    all_gather x1, blocking collectives, body(): group_grad = lax.all_gather(grad_out, 'tensor', axis=0, tiled=True)  34.8 us
    all_to_all x1, waiting for transfers between devices, body(): lax.all_to_all(backward, 'expert', split_axis=0, concat_axis=0, tiled=True)  23.4 us
    all_to_all x1, waiting for transfers between devices, send_routed(): lax.all_to_all(outgoing, 'expert', split_axis=0, concat_axis=0, tiled=True)  20.5 us
    all_to_all x1, starting transfers between devices, send_routed(): lax.all_to_all(outgoing, 'expert', split_axis=0, concat_axis=0, tiled=True)  13.6 us
    all_gather x1, waiting for transfers between devices, dense_branch(): lax.all_gather(dense_w_gate, 'expert', axis=0, tiled=True)  13.6 us
    all_to_all x1, starting transfers between devices, body(): lax.all_to_all(backward, 'expert', split_axis=0, concat_axis=0, tiled=True)  6.91 us
  transfers between devices with their start and end apart: 5, of which 5 were waited for; matrix products, arithmetic and copies ran while one was open for 7% of the time, Pallas kernels for 0%

commit v1 on v0

v1 whole, which is shorter than its diff:
```python
import functools
import math

import jax
import jax.numpy as jnp
from jax import lax
from jax.experimental import pallas as pl
from jax.experimental.pallas import tpu as pltpu
from jax.sharding import PartitionSpec as P

BF = jnp.bfloat16
F32 = jnp.float32
NT = (((1,), (1,)), ((), ()))
TN = (((0,), (0,)), ((), ()))
NN = (((1,), (0,)), ((), ()))


def mod(value, n):
    return lax.rem(value + 4 * n, n)


def dot(a, b, dims):
    return lax.dot_general(a, b, dims, preferred_element_type=F32)


def swiglu_back(upstream, gate_pre, up_pre):
    gate = gate_pre.astype(F32)
    up = up_pre.astype(F32)
    sigma = 1.0 / (1.0 + jnp.exp(-gate))
    grad_gate = upstream * up * (sigma * (1.0 + gate * (1.0 - sigma)))
    grad_up = upstream * (gate * sigma)
    return grad_gate.astype(BF), grad_up.astype(BF)


def kernel(
    NX, NY, NZ, C,
    grad, routes, probs, dgp, dup, dwg, dwu, dwd, egp, eup, ewg, ewu, ewd,
    out,
    xg, xf, xb, rt, pr, dgp_v, dup_v, dwd_v, egp_v, eup_v, ewd_v, ewg_v, ewu_v,
    wg, wf, gg, do_s, do_r, rf, s2, r2, s6, r6, ag, bk, rr, rs, s8, r8, tot,
    ld_sem, p1_s, p1_r, wz_s, wz_r, sib, gg_s, gg_r, do_ss, do_rs,
    p2_s, p2_r, p6_s, p6_r, ag_s, ag_r, rs_s, rs_r, p8_s, p8_r,
):
    T, D = grad.shape
    G = NX * T
    F = dwd.shape[0]
    RB = ag.shape[1]
    CW = D // C
    DB = do_s.shape[2]
    DR = dwg.shape[0]
    SL = NY * RB

    dp = lax.axis_index("dp")
    ex = lax.axis_index("expert")
    m = lax.axis_index("tensor")
    y = ex // NZ
    z = ex % NZ

    def rcopy(src, dst, ss, rsem, device):
        return pltpu.make_async_remote_copy(
            src_ref=src, dst_ref=dst, send_sem=ss, recv_sem=rsem,
            device_id=device, device_id_type=pl.DeviceIdType.MESH,
        )

    def at_x(x):
        return (dp, ex, x)

    def at_yz(yy, zz):
        return (dp, yy * NZ + zz, m)

    sibling = (1 - dp, ex, m)
    own_pair = mod(m + z, NY) == 0
    other_pair = jnp.logical_not(own_pair)

    loads = [
        pltpu.make_async_copy(grad, xg.at[m], ld_sem.at[0]),
        pltpu.make_async_copy(routes, rt, ld_sem.at[1]),
        pltpu.make_async_copy(probs, pr, ld_sem.at[2]),
        pltpu.make_async_copy(dwd, dwd_v, ld_sem.at[3]),
        pltpu.make_async_copy(dgp, dgp_v, ld_sem.at[4]),
        pltpu.make_async_copy(dup, dup_v, ld_sem.at[5]),
        pltpu.make_async_copy(ewd.at[0], ewd_v, ld_sem.at[6]),
        pltpu.make_async_copy(egp.at[0], egp_v, ld_sem.at[7]),
        pltpu.make_async_copy(eup.at[0], eup_v, ld_sem.at[8]),
        pltpu.make_async_copy(ewg.at[0], ewg_v, ld_sem.at[9]),
        pltpu.make_async_copy(ewu.at[0], ewu_v, ld_sem.at[10]),
    ]
    own_gate = pltpu.make_async_copy(dwg, wg.at[0, z], ld_sem.at[11])
    own_up = pltpu.make_async_copy(dwu, wg.at[1, z], ld_sem.at[11])

    @pl.when(dp == 0)
    def _():
        own_gate.start()

    @pl.when(dp == 1)
    def _():
        own_up.start()

    for load in loads:
        load.start()

    barrier = pltpu.get_barrier_semaphore()

    def greet(device):
        pl.semaphore_signal(barrier, inc=1, device_id=device, device_id_type=pl.DeviceIdType.MESH)

    for k in range(1, NX):
        greet(at_x(mod(m + k, NX)))
    for k in range(1, NY):
        greet(at_yz(mod(y + k, NY), z))
    for k in range(1, NZ):
        greet(at_yz(y, mod(z + k, NZ)))
    greet(sibling)

    def out_peer(k):
        zz = mod(z + k, NZ)
        return at_yz(mod(y + m + zz, NY), zz)

    def in_peer(k):
        return at_yz(mod(y - m - z, NY), mod(z + k, NZ))

    for k in range(1, NZ):
        greet(out_peer(k))
        greet(in_peer(k))

    @pl.when(other_pair)
    def _():
        greet(out_peer(0))
        greet(in_peer(0))

    fixed = NX - 1 + NY - 1 + NZ - 1 + 1 + 2 * (NZ - 1)
    pl.semaphore_wait(barrier, fixed + 2 * other_pair.astype(jnp.int32))

    sent = []

    p1 = []
    for k in range(1, NX):
        copy = rcopy(grad, xg.at[m], p1_s.at[k], p1_r.at[k], at_x(mod(m + k, NX)))
        copy.start()
        sent.append(copy)
    pltpu.make_async_copy(dwg, wg.at[0, z], ld_sem.at[11]).wait()
    for k in range(1, NZ):
        copy = rcopy(wg.at[dp, z], wg.at[dp, z], wz_s.at[k], wz_r.at[k], at_yz(y, mod(z + k, NZ)))
        copy.start()
        sent.append(copy)

    loads[1].wait()
    loads[2].wait()
    col = lax.broadcasted_iota(jnp.int32, (G, RB), 1)
    zc = lax.shift_right_logical(col, 1)
    named = jnp.bitwise_and(y + m + zc, NY - 1) * NZ + zc
    r0 = rt[:, 0:1]
    r1 = rt[:, 1:2]
    hit0 = (r0 == named).astype(F32)
    hit1 = (r1 == named).astype(F32)
    hits = hit0 + hit1
    below = (
        lax.broadcasted_iota(jnp.int32, (G, G), 0) > lax.broadcasted_iota(jnp.int32, (G, G), 1)
    ).astype(BF)
    rank = dot(below, hits.astype(BF), NN)
    taken = (rank == jnp.bitwise_and(col, 1).astype(F32)).astype(F32)
    select = (hits * taken).astype(BF)
    pv = pr[...].astype(F32)
    weights = ((hit0 * pv[:, 0:1] + hit1 * pv[:, 1:2]) * taken).astype(BF)

    loads[0].wait()
    for k in range(1, NX):
        rcopy(grad, xg.at[mod(m - k, NX)], p1_s.at[k], p1_r.at[k], at_x(mod(m - k, NX))).wait_recv()
    for j in range(NX):
        xf[j * T:(j + 1) * T, :] = xg[j].astype(F32)
    xb[...] = xf[...].astype(BF)

    rf[...] = dot(select, xb[...], TN)
    for j in range(NZ):
        s2[j] = rf[2 * j:2 * j + 2, :].astype(BF)

    def exchange(src, dst, ssem, rsem, peer):
        local = pltpu.make_async_copy(src.at[z], dst.at[z], rsem.at[0])

        @pl.when(own_pair)
        def _():
            local.start()

        first = rcopy(src.at[z], dst.at[z], ssem.at[0], rsem.at[0], peer(0))

        @pl.when(other_pair)
        def _():
            first.start()

        for k in range(1, NZ):
            copy = rcopy(src.at[mod(z + k, NZ)], dst.at[z], ssem.at[k], rsem.at[k], peer(k))
            copy.start()
            sent.append(copy)
        return first

    def arrive(src, dst, ssem, rsem, peer):
        for k in range(NZ):
            rcopy(src.at[0], dst.at[mod(z - k, NZ)], ssem.at[k], rsem.at[k], peer(k)).wait_recv()

    p2_first = exchange(s2, r2, p2_s, p2_r, out_peer)

    loads[3].wait()
    loads[4].wait()
    loads[5].wait()
    dense_up = dot(xb[...], dwd_v[...], NT)
    dense_gg, dense_gu = swiglu_back(dense_up, dgp_v[...], dup_v[...])
    gg[y, 0] = dense_gg
    gg[y, 1] = dense_gu

    arrive(s2, r2, p2_s, p2_r, out_peer)
    for j in range(NZ):
        rf[2 * j:2 * j + 2, :] = r2[j].astype(F32)

    def block_of(member):
        return mod(y - z - member, NY)

    mine = block_of(m)
    ag[mine] = rf[...].astype(BF)

    right = at_x(mod(m + 1, NX))
    left = at_x(mod(m - 1, NX))
    far = NX // 2
    near = NX - 1 - far
    hops = [(far, near) if c % 2 == 0 else (near, far) for c in range(C)]

    def cols(c):
        return pl.ds(c * CW, CW)

    def ag_copy(d, t, c):
        step = t if d == 0 else -t
        ref = ag.at[block_of(m - step), :, cols(c)]
        return rcopy(ref, ref, ag_s.at[d, t, c], ag_r.at[d, t, c], (right, left)[d])

    def ag_arrival(d, t, c):
        step = t + 1 if d == 0 else -(t + 1)
        ref = ag.at[block_of(m - step), :, cols(c)]
        rcopy(ref, ref, ag_s.at[d, t, c], ag_r.at[d, t, c], (right, left)[d]).wait_recv()

    for c in range(C):
        for d in range(2):
            if hops[c][d] > 0:
                copy = ag_copy(d, 0, c)
                copy.start()
                sent.append(copy)

    for k in range(1, NY):
        copy = rcopy(gg.at[y], gg.at[y], gg_s.at[k], gg_r.at[k], at_yz(mod(y + k, NY), z))
        copy.start()
        sent.append(copy)
    for k in range(1, NZ):
        rcopy(
            wg.at[dp, z], wg.at[dp, mod(z - k, NZ)], wz_s.at[k], wz_r.at[k], at_yz(y, mod(z + k, NZ))
        ).wait_recv()
    to_sibling = rcopy(wg.at[dp], wg.at[dp], sib.at[0], sib.at[1], sibling)
    to_sibling.start()
    sent.append(to_sibling)

    loads[6].wait()
    for t in range(1, far):
        for c in range(C):
            for d in range(2):
                if t < hops[c][d]:
                    ag_arrival(d, t - 1, c)
                    copy = ag_copy(d, t, c)
                    copy.start()
                    sent.append(copy)
    upstream = jnp.zeros((SL, F), F32)
    for c in range(C):
        for d in range(2):
            if hops[c][d] > 0:
                ag_arrival(d, hops[c][d] - 1, c)
        rows = ag[:, :, c * CW:(c + 1) * CW].reshape(SL, CW)
        upstream = upstream + dot(rows, ewd_v[:, c * CW:(c + 1) * CW], NT)
    loads[7].wait()
    loads[8].wait()
    expert_gg, expert_gu = swiglu_back(upstream, egp_v[...], eup_v[...])

    def rs_copy(d, t, c):
        goal = m + hops[c][0] - t if d == 0 else m - hops[c][1] + t
        src = bk.at[block_of(goal), :, cols(c)] if t == 0 else rs.at[d, t, :, cols(c)]
        return rcopy(src, rr.at[d, t, :, cols(c)], rs_s.at[d, t, c], rs_r.at[d, t, c], (right, left)[d])

    def rs_arrival(d, t, c):
        rcopy(
            bk.at[0, :, cols(c)], rr.at[d, t, :, cols(c)], rs_s.at[d, t, c], rs_r.at[d, t, c], (right, left)[d]
        ).wait_recv()

    loads[9].wait()
    loads[10].wait()
    for c in range(C):
        span = slice(c * CW, (c + 1) * CW)
        back = dot(expert_gg, ewg_v[span, :], NT) + dot(expert_gu, ewu_v[span, :], NT)
        bk[:, :, span] = back.astype(BF).reshape(NY, RB, CW)
        for d in range(2):
            if hops[c][d] > 0:
                copy = rs_copy(d, 0, c)
                copy.start()
                sent.append(copy)

    for k in range(1, NY):
        rcopy(
            gg.at[y], gg.at[mod(y - k, NY)], gg_s.at[k], gg_r.at[k], at_yz(mod(y + k, NY), z)
        ).wait_recv()
    rcopy(wg.at[1 - dp], wg.at[1 - dp], sib.at[0], sib.at[1], sibling).wait_recv()
    dense = jnp.zeros((NY * G, DB), F32)
    for which in range(2):
        for j in range(NZ):
            wf[which, j * DR:(j + 1) * DR, :] = wg[which, j].astype(F32)
        dense = dense + dot(gg[:, which].reshape(NY * G, F), wf[which].astype(BF), NT)
    do_s[...] = dense.astype(BF).reshape(NY, G, DB)
    for k in range(1, NY):
        goal = mod(y + k, NY)
        copy = rcopy(do_s.at[goal], do_r.at[y], do_ss.at[k], do_rs.at[k], at_yz(goal, z))
        copy.start()
        sent.append(copy)
    do_r[y] = do_s[y]

    for t in range(1, far):
        for c in range(C):
            span = slice(c * CW, (c + 1) * CW)
            for d in range(2):
                if t < hops[c][d]:
                    rs_arrival(d, t - 1, c)
                    goal = m + hops[c][0] - t if d == 0 else m - hops[c][1] + t
                    part = rr[d, t - 1, :, span].astype(F32) + bk[block_of(goal), :, span].astype(F32)
                    rs[d, t, :, span] = part.astype(BF)
                    copy = rs_copy(d, t, c)
                    copy.start()
                    sent.append(copy)
    for c in range(C):
        span = slice(c * CW, (c + 1) * CW)
        part = bk[mine, :, span].astype(F32)
        for d in range(2):
            if hops[c][d] > 0:
                rs_arrival(d, hops[c][d] - 1, c)
                part = part + rr[d, hops[c][d] - 1, :, span].astype(F32)
        rf[:, span] = part
    for j in range(NZ):
        s6[j] = rf[2 * j:2 * j + 2, :].astype(BF)

    p6_first = exchange(s6, r6, p6_s, p6_r, in_peer)

    for k in range(1, NY):
        rcopy(
            do_s.at[y], do_r.at[mod(y - k, NY)], do_ss.at[k], do_rs.at[k], at_yz(mod(y + k, NY), z)
        ).wait_recv()
    pair = 2 if (2 * DB) % 128 == 0 and NY % 2 == 0 else NY
    for j in range(0, NY, pair):
        tot[:, j * DB:(j + pair) * DB] = jnp.concatenate(
            [do_r[j + i].astype(F32) for i in range(pair)], axis=1
        )

    arrive(s6, r6, p6_s, p6_r, in_peer)
    for j in range(NZ):
        rf[2 * j:2 * j + 2, :] = r6[j].astype(F32)
    tot[...] = tot[...] + dot(weights, rf[...].astype(BF), NN)

    for j in range(NX):
        s8[j] = tot[j * T:(j + 1) * T, :].astype(BF)
    for k in range(1, NX):
        goal = mod(m + k, NX)
        copy = rcopy(s8.at[goal], r8.at[m], p8_s.at[k], p8_r.at[k], at_x(goal))
        copy.start()
        sent.append(copy)
    total = xg[m].astype(F32) + s8[m].astype(F32)
    for k in range(1, NX):
        source = mod(m - k, NX)
        rcopy(s8.at[0], r8.at[source], p8_s.at[k], p8_r.at[k], at_x(source)).wait_recv()
        total = total + r8[source].astype(F32)
    out[...] = total.astype(BF)

    for copy in sent:
        copy.wait_send()

    @pl.when(other_pair)
    def _():
        p2_first.wait_send()
        p6_first.wait_send()


def body(NX, NY, NZ, *args):
    grad, routes, probs, dgp, dup, dwg, dwu, dwd, egp, eup, ewg, ewu, ewd = args
    T, D = grad.shape
    G = NX * T
    F = dwd.shape[0]
    SL = egp.shape[1]
    RB = SL // NY
    DR = dwg.shape[0]
    DB = DR * NZ
    C = 4
    far = NX // 2
    V = pltpu.VMEM
    dma = pltpu.SemaphoreType.DMA
    scratch = [
        V((NX, T, D), BF), V((G, D), F32), V((G, D), BF), V((G, 2), jnp.int32), V((G, 2), BF),
        V((G, F), BF), V((G, F), BF), V((F, D), BF), V((SL, F), BF), V((SL, F), BF),
        V((F, D), BF), V((D, F), BF), V((D, F), BF),
        V((2, NZ, DR, F), BF), V((2, DB, F), F32), V((NY, 2, G, F), BF),
        V((NY, G, DB), BF), V((NY, G, DB), BF), V((RB, D), F32),
        V((NZ, 2, D), BF), V((NZ, 2, D), BF), V((NZ, 2, D), BF), V((NZ, 2, D), BF),
        V((NY, RB, D), BF), V((NY, RB, D), BF),
        V((2, far, RB, D), BF), V((2, far, RB, D), BF),
        V((NX, T, D), BF), V((NX, T, D), BF), V((G, D), F32),
        dma((12,)), dma((NX,)), dma((NX,)), dma((NZ,)), dma((NZ,)), dma((2,)),
        dma((NY,)), dma((NY,)), dma((NY,)), dma((NY,)),
        dma((NZ,)), dma((NZ,)), dma((NZ,)), dma((NZ,)),
        dma((2, far, C)), dma((2, far, C)), dma((2, far, C)), dma((2, far, C)),
        dma((NX,)), dma((NX,)),
    ]
    flops = 2 * 3 * F * D * (SL + G)
    return pl.pallas_call(
        functools.partial(kernel, NX, NY, NZ, C),
        out_shape=jax.ShapeDtypeStruct((T, D), BF),
        in_specs=[pl.BlockSpec(memory_space=pl.ANY)] * 13,
        out_specs=pl.BlockSpec(memory_space=pltpu.VMEM),
        scratch_shapes=scratch,
        compiler_params=pltpu.CompilerParams(
            collective_id=0, has_side_effects=True, vmem_limit_bytes=48 * 1024 * 1024
        ),
        cost_estimate=pl.CostEstimate(
            flops=flops, bytes_accessed=8 * F * D, transcendentals=F * (SL + G)
        ),
        name="layer_back",
    )(*args)


def solution(mesh):
    NX = mesh.shape["tensor"]
    NE = mesh.shape["expert"]
    NY = NX
    NZ = NE // NY
    return jax.shard_map(
        functools.partial(body, NX, NY, NZ),
        mesh=mesh,
        in_specs=(
            P(("dp", "expert", "tensor"), None),
            P(("dp", "expert"), None),
            P(("dp", "expert"), None),
            P(("dp", "expert"), "tensor"),
            P(("dp", "expert"), "tensor"),
            P("expert", "tensor"),
            P("expert", "tensor"),
            P("tensor", None),
            P(("dp", "expert"), None, "tensor"),
            P(("dp", "expert"), None, "tensor"),
            P("expert", None, "tensor"),
            P("expert", None, "tensor"),
            P("expert", "tensor", None),
        ),
        out_specs=P(("dp", "expert", "tensor"), None),
        check_vma=False,
    )
```

time: 326 us -> 103 us (0.32)
  waiting for transfers between devices: 228 us -> 0 us
  Pallas kernels: 0 us -> 86.9 us
  blocking collectives: 34.8 us -> 0 us
  starting transfers between devices: 20.6 us -> 0 us
  matrix products: 13.9 us -> 0 us
  between operations: 13.9 us -> 0.08 us
  local copies, waits for them, and re-layouts: 9.65 us -> 14.7 us
  other arithmetic: 3.87 us -> 0 us
    all_gather x2 -> x0, waiting for transfers between devices: 106 us -> none  [the longest x1 91.9 us: dense_branch(): lax.all_gather(dense_w_up, 'expert', axis=0, tiled=True)]
    pallas_call x0 -> x1, Pallas kernels: none -> 86.9 us  [body(): pl.pallas_call(functools.partial(kernel, NX, NY, NZ, C), out_shape=jax.Sh...]
    unnamed x4 -> x0, waiting for transfers between devices: 79 us -> none
    all_to_all x2 -> x0, waiting for transfers between devices: 43.9 us -> none  [the longest x1 23.4 us: body(): lax.all_to_all(backward, 'expert', split_axis=0, concat_axis=0, tiled=True)]
    all_gather x1 -> x0, blocking collectives: 34.8 us -> none  [body(): group_grad = lax.all_gather(grad_out, 'tensor', axis=0, tiled=True)]
    all_to_all x2 -> x0, starting transfers between devices: 20.6 us -> none  [the longest x1 13.6 us: send_routed(): lax.all_to_all(outgoing, 'expert', split_axis=0, concat_axis=0, tiled=True)]
    dot_general x8 -> x0, matrix products: 13.9 us -> none  [the longest x1 2.97 us: dense_branch(): jnp.einsum('td,fd->tf', group_grad, dense_w_down, preferred_element_type=...]
    unnamed x13 -> x21, local copies, waits for them, and re-layouts: 3 us -> 14.7 us
  transfers between devices with their start and end apart: 5 -> 0, of which waited for: 5 -> 0; matrix products, arithmetic and copies ran while one was open for 7% -> 0% of each run, Pallas kernels for 0% -> 0%
where the time goes in v1:
time: 103 us; the launch traced here: 102 us
  Pallas kernels  86.9 us (84%)
  local copies, waits for them, and re-layouts  14.7 us (14%)
    pallas_call x1, Pallas kernels, body(): pl.pallas_call(functools.partial(kernel, NX, NY, NZ, C), out_shape=jax.Sh...  86.9 us
    unnamed x21, local copies, waits for them, and re-layouts  14.7 us

profile of v1, /device:TPU:14, one launch (start us, length us, event | category | flops | bytes accessed | tf_op | source)
XLA Modules:
  0.0 101.6 jit_solution(12998127423248509093)
XLA Ops:
  0.0 0.7 copy.15.probs
  0.7 0.8 copy.14.routes
  1.5 1.0 copy.16.egp
  2.5 1.0 copy.17.eup
  3.5 4.4 %copy.18.ewg = bf16[1,3584,304]{2,1,0:T(8,128)(2,1)} copy(bf16[1,3584,304]{1,2,0:T(8,128)(2,1)} %param.23) | data formatting | bytes 4358144 | tf_op args[10]
  7.9 0.0 copy-start
  7.9 0.0 copy-start.2
  7.9 0.0 copy-start.3
  7.9 0.0 copy-start.4
  7.9 0.0 copy-start.5
  8.0 0.0 copy-start.6
  8.0 4.5 %copy.19.ewu = bf16[1,3584,304]{2,1,0:T(8,128)(2,1)} copy(bf16[1,3584,304]{1,2,0:T(8,128)(2,1)} %param.24) | data formatting | bytes 4358144 | tf_op args[11]
  12.5 0.0 copy-done
  12.5 0.0 copy-done.2
  12.5 0.0 copy-done.3
  12.5 0.0 copy-done.4
  12.5 0.0 copy-done.5
  12.5 0.0 copy-done.6
  12.5 0.0 copy-start.1
  12.6 1.6 %copy-done.1 = bf16[1,304,3584]{2,1,0:T(8,128)(2,1)S(1)} copy-done((bf16[1,304,3584]{2,1,0:T(8,128)(2,1)S(1)}, bf16[1,304,3584]{2,1,0:T(8,128)(2,1)}, u32[]{:S(2)}) %copy-start.1) | copy-done | bytes 2179096
  14.2 86.9 %layer_back.1 = bf16[4,3584]{1,0:T(4,128)(2,1)S(1)} custom-call(bf16[4,3584]{1,0:T(4,128)(2,1)S(1)} %copy-done.4, s32[32,2]{1,0:T(8,128)S(1)} %copy.14.routes, bf16[32,2]{1,0:T(8,128)(2,1)S(1)} %copy.15.probs, bf16[32,304]{1,0:T(8,128)(2,1)S(1)} %copy-done.5, bf16[32,304]{1,0:T(8,128)(2,1)S(1)} %copy-done.6, bf16[56,304]{1,0:T(8,128)(2,1)S(1)} %copy-done.2, ...), custom_call_target="tpu_custom_call" | custom-call | flops 1045954560 | bytes 8716288 | tf_op jit(solution)/shard_map/layer_back/pallas_call | solution.py:411
  101.0 0.6 copy.21
Async XLA Ops:
  7.9 4.6 %copy-start = (bf16[304,3584]{1,0:T(8,128)(2,1)S(1)}, bf16[304,3584]{1,0:T(8,128)(2,1)}, u32[]{:S(2)}) copy-start(bf16[304,3584]{1,0:T(8,128)(2,1)} %dwd.1) | copy-start | bytes 6537220
  7.9 4.6 %copy-start.2 = (bf16[56,304]{1,0:T(8,128)(2,1)S(1)}, bf16[56,304]{1,0:T(8,128)(2,1)}, u32[]{:S(2)}) copy-start(bf16[56,304]{1,0:T(8,128)(2,1)} %dwg.1) | copy-start | bytes 102148
  7.9 4.6 %copy-start.3 = (bf16[56,304]{1,0:T(8,128)(2,1)S(1)}, bf16[56,304]{1,0:T(8,128)(2,1)}, u32[]{:S(2)}) copy-start(bf16[56,304]{1,0:T(8,128)(2,1)} %dwu.1) | copy-start | bytes 102148
  7.9 4.6 %copy-start.4 = (bf16[4,3584]{1,0:T(4,128)(2,1)S(1)}, bf16[4,3584]{1,0:T(4,128)(2,1)}, u32[]{:S(2)}) copy-start(bf16[4,3584]{1,0:T(4,128)(2,1)} %grad.1) | copy-start | bytes 86020
  7.9 4.6 %copy-start.5 = (bf16[32,304]{1,0:T(8,128)(2,1)S(1)}, bf16[32,304]{1,0:T(8,128)(2,1)}, u32[]{:S(2)}) copy-start(bf16[32,304]{1,0:T(8,128)(2,1)} %dgp.1) | copy-start | bytes 58372
  8.0 4.6 %copy-start.6 = (bf16[32,304]{1,0:T(8,128)(2,1)S(1)}, bf16[32,304]{1,0:T(8,128)(2,1)}, u32[]{:S(2)}) copy-start(bf16[32,304]{1,0:T(8,128)(2,1)} %dup.1) | copy-start | bytes 58372
  12.5 1.6 %copy-start.1 = (bf16[1,304,3584]{2,1,0:T(8,128)(2,1)S(1)}, bf16[1,304,3584]{2,1,0:T(8,128)(2,1)}, u32[]{:S(2)}) copy-start(bf16[1,304,3584]{2,1,0:T(8,128)(2,1)} %ewd.1) | copy-start | bytes 6537220

commit v2 on v1

--- a/solution.py
+++ b/solution.py
@@ -29,7 +29,7 @@
     sigma = 1.0 / (1.0 + jnp.exp(-gate))
     grad_gate = upstream * up * (sigma * (1.0 + gate * (1.0 - sigma)))
     grad_up = upstream * (gate * sigma)
-    return grad_gate.astype(BF), grad_up.astype(BF)
+    return grad_gate, grad_up
 
 
 def kernel(
@@ -146,22 +146,22 @@
 
     loads[1].wait()
     loads[2].wait()
-    col = lax.broadcasted_iota(jnp.int32, (G, RB), 1)
-    zc = lax.shift_right_logical(col, 1)
+    slot = lax.broadcasted_iota(jnp.int32, (RB, G), 0)
+    zc = lax.shift_right_logical(slot, 1)
     named = jnp.bitwise_and(y + m + zc, NY - 1) * NZ + zc
-    r0 = rt[:, 0:1]
-    r1 = rt[:, 1:2]
+    r0 = rt[0:1, :]
+    r1 = rt[1:2, :]
     hit0 = (r0 == named).astype(F32)
     hit1 = (r1 == named).astype(F32)
     hits = hit0 + hit1
-    below = (
-        lax.broadcasted_iota(jnp.int32, (G, G), 0) > lax.broadcasted_iota(jnp.int32, (G, G), 1)
+    earlier = (
+        lax.broadcasted_iota(jnp.int32, (G, G), 0) < lax.broadcasted_iota(jnp.int32, (G, G), 1)
     ).astype(BF)
-    rank = dot(below, hits.astype(BF), NN)
-    taken = (rank == jnp.bitwise_and(col, 1).astype(F32)).astype(F32)
+    rank = dot(hits.astype(BF), earlier, NN)
+    taken = (rank == jnp.bitwise_and(slot, 1).astype(F32)).astype(F32)
     select = (hits * taken).astype(BF)
     pv = pr[...].astype(F32)
-    weights = ((hit0 * pv[:, 0:1] + hit1 * pv[:, 1:2]) * taken).astype(BF)
+    weights = ((hit0 * pv[0:1, :] + hit1 * pv[1:2, :]) * taken).astype(BF)
 
     loads[0].wait()
     for k in range(1, NX):
@@ -170,7 +170,7 @@
         xf[j * T:(j + 1) * T, :] = xg[j].astype(F32)
     xb[...] = xf[...].astype(BF)
 
-    rf[...] = dot(select, xb[...], TN)
+    rf[...] = dot(select, xb[...], NN)
     for j in range(NZ):
         s2[j] = rf[2 * j:2 * j + 2, :].astype(BF)
 
@@ -204,8 +204,8 @@
     loads[5].wait()
     dense_up = dot(xb[...], dwd_v[...], NT)
     dense_gg, dense_gu = swiglu_back(dense_up, dgp_v[...], dup_v[...])
-    gg[y, 0] = dense_gg
-    gg[y, 1] = dense_gu
+    gg[y, 0] = dense_gg.astype(BF)
+    gg[y, 1] = dense_gu.astype(BF)
 
     arrive(s2, r2, p2_s, p2_r, out_peer)
     for j in range(NZ):
@@ -264,16 +264,18 @@
                     copy = ag_copy(d, t, c)
                     copy.start()
                     sent.append(copy)
-    upstream = jnp.zeros((SL, F), F32)
+    upstream = jnp.zeros((F, SL), F32)
     for c in range(C):
         for d in range(2):
             if hops[c][d] > 0:
                 ag_arrival(d, hops[c][d] - 1, c)
         rows = ag[:, :, c * CW:(c + 1) * CW].reshape(SL, CW)
-        upstream = upstream + dot(rows, ewd_v[:, c * CW:(c + 1) * CW], NT)
+        upstream = upstream + dot(ewd_v[:, c * CW:(c + 1) * CW], rows, NT)
     loads[7].wait()
     loads[8].wait()
-    expert_gg, expert_gu = swiglu_back(upstream, egp_v[...], eup_v[...])
+    expert_gg, expert_gu = [
+        jnp.transpose(part).astype(BF) for part in swiglu_back(upstream, egp_v[...], eup_v[...])
+    ]
 
     def rs_copy(d, t, c):
         goal = m + hops[c][0] - t if d == 0 else m - hops[c][1] + t
@@ -289,7 +291,7 @@
     loads[10].wait()
     for c in range(C):
         span = slice(c * CW, (c + 1) * CW)
-        back = dot(expert_gg, ewg_v[span, :], NT) + dot(expert_gu, ewu_v[span, :], NT)
+        back = dot(expert_gg, ewg_v[:, span], NN) + dot(expert_gu, ewu_v[:, span], NN)
         bk[:, :, span] = back.astype(BF).reshape(NY, RB, CW)
         for d in range(2):
             if hops[c][d] > 0:
@@ -353,7 +355,7 @@
     arrive(s6, r6, p6_s, p6_r, in_peer)
     for j in range(NZ):
         rf[2 * j:2 * j + 2, :] = r6[j].astype(F32)
-    tot[...] = tot[...] + dot(weights, rf[...].astype(BF), NN)
+    tot[...] = tot[...] + dot(weights, rf[...].astype(BF), TN)
 
     for j in range(NX):
         s8[j] = tot[j * T:(j + 1) * T, :].astype(BF)
@@ -384,6 +386,8 @@
     G = NX * T
     F = dwd.shape[0]
     SL = egp.shape[1]
+    routes, probs = routes.T, probs.T
+    egp, eup, ewg, ewu = [jnp.swapaxes(part, 1, 2) for part in (egp, eup, ewg, ewu)]
     RB = SL // NY
     DR = dwg.shape[0]
     DB = DR * NZ
@@ -392,9 +396,9 @@
     V = pltpu.VMEM
     dma = pltpu.SemaphoreType.DMA
     scratch = [
-        V((NX, T, D), BF), V((G, D), F32), V((G, D), BF), V((G, 2), jnp.int32), V((G, 2), BF),
-        V((G, F), BF), V((G, F), BF), V((F, D), BF), V((SL, F), BF), V((SL, F), BF),
-        V((F, D), BF), V((D, F), BF), V((D, F), BF),
+        V((NX, T, D), BF), V((G, D), F32), V((G, D), BF), V((2, G), jnp.int32), V((2, G), BF),
+        V((G, F), BF), V((G, F), BF), V((F, D), BF), V((F, SL), BF), V((F, SL), BF),
+        V((F, D), BF), V((F, D), BF), V((F, D), BF),
         V((2, NZ, DR, F), BF), V((2, DB, F), F32), V((NY, 2, G, F), BF),
         V((NY, G, DB), BF), V((NY, G, DB), BF), V((RB, D), F32),
         V((NZ, 2, D), BF), V((NZ, 2, D), BF), V((NZ, 2, D), BF), V((NZ, 2, D), BF),
@@ -415,13 +419,13 @@
         out_specs=pl.BlockSpec(memory_space=pltpu.VMEM),
         scratch_shapes=scratch,
         compiler_params=pltpu.CompilerParams(
-            collective_id=0, has_side_effects=True, vmem_limit_bytes=48 * 1024 * 1024
+            collective_id=0, has_side_effects=True, vmem_limit_bytes=62 * 1024 * 1024
         ),
         cost_estimate=pl.CostEstimate(
             flops=flops, bytes_accessed=8 * F * D, transcendentals=F * (SL + G)
         ),
         name="layer_back",
-    )(*args)
+    )(grad, routes, probs, dgp, dup, dwg, dwu, dwd, egp, eup, ewg, ewu, ewd)
 
 
 def solution(mesh):

time: 103 us -> 88.6 us (0.86)
  local copies, waits for them, and re-layouts: 14.7 us -> 1.37 us
  Pallas kernels: 86.9 us -> 85.8 us
    unnamed x21 -> x1, local copies, waits for them, and re-layouts: 14.7 us -> 1.37 us
where the time goes in v2:
time: 88.6 us; the launch traced here: 87.2 us
  Pallas kernels  85.8 us (97%)
  local copies, waits for them, and re-layouts  1.37 us (2%)
    pallas_call x1, Pallas kernels, body(): pl.pallas_call(functools.partial(kernel, NX, NY, NZ, C), out_shape=jax.Sh...  85.8 us

profile of v2, /device:TPU:14, one launch (start us, length us, event | category | flops | bytes accessed | tf_op | source)
XLA Modules:
  0.0 87.2 jit_solution(14863614574565013661)
XLA Ops:
  0.0 85.8 %layer_back.1 = bf16[4,3584]{1,0:T(4,128)(2,1)} custom-call(bf16[4,3584]{1,0:T(4,128)(2,1)} %grad.1, s32[2,32]{1,0:T(2,128)} %bitcast.10, bf16[2,32]{1,0:T(2,128)(2,1)} %bitcast.11, bf16[32,304]{1,0:T(8,128)(2,1)} %dgp.1, bf16[32,304]{1,0:T(8,128)(2,1)} %dup.1, bf16[56,304]{1,0:T(8,128)(2,1)} %dwg.1, bf16[56,304]{1,0:T(8,128)(2,1)} %dwu.1, ...), custom_call_target="tpu_custom_call" | custom-call | flops 1045954560 | bytes 8716288 | tf_op jit(solution)/shard_map/layer_back/pallas_call | solution.py:415
  85.9 1.4 %copy.15 = bf16[4,3584]{1,0:T(4,128)(2,1)} copy(bf16[4,3584]{1,0:T(4,128)(2,1)} %layer_back.1) | data formatting | bytes 57344

commit v3 on v2

v3 whole, which is shorter than its diff:
```python
import functools
import math

import jax
import jax.numpy as jnp
from jax import lax
from jax.experimental import pallas as pl
from jax.experimental.pallas import tpu as pltpu
from jax.sharding import PartitionSpec as P

BF = jnp.bfloat16
F32 = jnp.float32
NT = (((1,), (1,)), ((), ()))
TN = (((0,), (0,)), ((), ()))
NN = (((1,), (0,)), ((), ()))


def mod(value, n):
    return lax.rem(value + 4 * n, n)


def dot(a, b, dims):
    return lax.dot_general(a, b, dims, preferred_element_type=F32)


def swiglu_back(upstream, gate_pre, up_pre):
    gate = gate_pre.astype(F32)
    up = up_pre.astype(F32)
    sigma = 1.0 / (1.0 + jnp.exp(-gate))
    grad_gate = upstream * up * (sigma * (1.0 + gate * (1.0 - sigma)))
    grad_up = upstream * (gate * sigma)
    return grad_gate, grad_up


def kernel(
    NX, NY, NZ, C,
    grad, routes, probs, dgp, dup, dwg, dwu, dwd, egp, eup, ewg, ewu, ewd,
    out,
    xg, xf, xb, rt, pr, dgp_v, dup_v, dwd_v, egp_v, eup_v, ewd_v, ewg_v, ewu_v,
    wg, wf, gg, do_s, do_r, rf, rg, s2, r2, s6, r6, ag, bk, rr, rs, s8, r8, tot,
    ld_sem, p1_s, p1_r, wz_s, wz_r, sib, gg_s, gg_r, do_ss, do_rs,
    p2_s, p2_r, p6_s, p6_r, ag_s, ag_r, rs_s, rs_r, p8_s, p8_r,
):
    T, D = grad.shape
    G = NX * T
    F = dwd.shape[0]
    RB = ag.shape[1]
    CW = D // C
    DB = do_s.shape[2]
    DR = dwg.shape[0]
    SL = NY * RB

    dp = lax.axis_index("dp")
    ex = lax.axis_index("expert")
    m = lax.axis_index("tensor")
    y = ex // NZ
    z = ex % NZ

    def rcopy(src, dst, ss, rsem, device):
        return pltpu.make_async_remote_copy(
            src_ref=src, dst_ref=dst, send_sem=ss, recv_sem=rsem,
            device_id=device, device_id_type=pl.DeviceIdType.MESH,
        )

    def at_x(x):
        return (dp, ex, x)

    def at_yz(yy, zz):
        return (dp, yy * NZ + zz, m)

    sibling = (1 - dp, ex, m)
    own_pair = mod(m + z, NY) == 0
    other_pair = jnp.logical_not(own_pair)

    barrier = pltpu.get_barrier_semaphore()

    def greet(device):
        pl.semaphore_signal(barrier, inc=1, device_id=device, device_id_type=pl.DeviceIdType.MESH)

    def out_peer(k):
        zz = mod(z + k, NZ)
        return at_yz(mod(y + m + zz, NY), zz)

    def in_peer(k):
        return at_yz(mod(y - m - z, NY), mod(z + k, NZ))

    for k in range(1, NX):
        greet(at_x(mod(m + k, NX)))
    for k in range(1, NZ):
        greet(in_peer(k))
        greet(out_peer(k))

    @pl.when(other_pair)
    def _():
        greet(in_peer(0))
        greet(out_peer(0))

    for k in range(1, NZ):
        greet(at_yz(y, mod(z + k, NZ)))
    for k in range(1, NY):
        greet(at_yz(mod(y + k, NY), z))
    greet(sibling)

    loads = [
        pltpu.make_async_copy(grad, xg.at[m], ld_sem.at[0]),
        pltpu.make_async_copy(routes, rt, ld_sem.at[1]),
        pltpu.make_async_copy(probs, pr, ld_sem.at[2]),
        pltpu.make_async_copy(dwd, dwd_v, ld_sem.at[3]),
        pltpu.make_async_copy(dgp, dgp_v, ld_sem.at[4]),
        pltpu.make_async_copy(dup, dup_v, ld_sem.at[5]),
        pltpu.make_async_copy(ewd.at[0], ewd_v, ld_sem.at[6]),
        pltpu.make_async_copy(egp.at[0], egp_v, ld_sem.at[7]),
        pltpu.make_async_copy(eup.at[0], eup_v, ld_sem.at[8]),
        pltpu.make_async_copy(ewg.at[0], ewg_v, ld_sem.at[9]),
        pltpu.make_async_copy(ewu.at[0], ewu_v, ld_sem.at[10]),
    ]
    own_gate = pltpu.make_async_copy(dwg, wg.at[0, z], ld_sem.at[11])
    own_up = pltpu.make_async_copy(dwu, wg.at[1, z], ld_sem.at[11])
    for load in loads[:3]:
        load.start()

    @pl.when(dp == 0)
    def _():
        own_gate.start()

    @pl.when(dp == 1)
    def _():
        own_up.start()

    for load in loads[3:]:
        load.start()

    fixed = NX - 1 + NY - 1 + NZ - 1 + 1 + 2 * (NZ - 1)
    pl.semaphore_wait(barrier, fixed + 2 * other_pair.astype(jnp.int32))

    sent = []

    def send(copy):
        copy.start()
        sent.append(copy)

    def flush():
        for copy in sent:
            copy.wait_send()
        sent.clear()

    H = 2
    HW = D // H

    def half(h):
        return pl.ds(h * HW, HW)

    def span(h):
        return slice(h * HW, (h + 1) * HW)

    order = sorted(range(1, NX), key=lambda k: -min(k, NX - k))

    for h in range(H):
        for k in order:
            send(rcopy(
                grad.at[:, half(h)], xg.at[m, :, half(h)], p1_s.at[h, k], p1_r.at[h, k], at_x(mod(m + k, NX))
            ))

    loads[1].wait()
    loads[2].wait()
    slot = lax.broadcasted_iota(jnp.int32, (RB, G), 0)
    zc = lax.shift_right_logical(slot, 1)
    named = jnp.bitwise_and(y + m + zc, NY - 1) * NZ + zc
    r0 = rt[0:1, :]
    r1 = rt[1:2, :]
    hit0 = (r0 == named).astype(F32)
    hit1 = (r1 == named).astype(F32)
    hits = hit0 + hit1
    earlier = (
        lax.broadcasted_iota(jnp.int32, (G, G), 0) < lax.broadcasted_iota(jnp.int32, (G, G), 1)
    ).astype(BF)
    rank = dot(hits.astype(BF), earlier, NN)
    taken = (rank == jnp.bitwise_and(slot, 1).astype(F32)).astype(F32)
    select = (hits * taken).astype(BF)
    pv = pr[...].astype(F32)
    weights = ((hit0 * pv[0:1, :] + hit1 * pv[1:2, :]) * taken).astype(BF)

    pltpu.make_async_copy(dwg, wg.at[0, z], ld_sem.at[11]).wait()
    for k in range(1, NZ):
        send(rcopy(wg.at[dp, z], wg.at[dp, z], wz_s.at[k], wz_r.at[k], at_yz(y, mod(z + k, NZ))))

    firsts = []

    def exchange(src, dst, ssem, rsem, peer, h):
        local = pltpu.make_async_copy(src.at[z, :, half(h)], dst.at[z, :, half(h)], rsem.at[h, 0])

        @pl.when(own_pair)
        def _():
            local.start()

        first = rcopy(
            src.at[z, :, half(h)], dst.at[z, :, half(h)], ssem.at[h, 0], rsem.at[h, 0], peer(0)
        )

        @pl.when(other_pair)
        def _():
            first.start()

        firsts.append(first)
        for k in range(1, NZ):
            send(rcopy(
                src.at[mod(z + k, NZ), :, half(h)], dst.at[z, :, half(h)], ssem.at[h, k], rsem.at[h, k], peer(k)
            ))

    def arrive(src, dst, ssem, rsem, peer, h):
        for k in range(NZ):
            rcopy(
                src.at[0, :, half(h)], dst.at[mod(z - k, NZ), :, half(h)], ssem.at[h, k], rsem.at[h, k], peer(k)
            ).wait_recv()

    loads[0].wait()
    for h in range(H):
        for k in order:
            source = mod(m - k, NX)
            rcopy(
                grad.at[:, half(h)], xg.at[source, :, half(h)], p1_s.at[h, k], p1_r.at[h, k], at_x(source)
            ).wait_recv()
        for j in range(NX):
            xf[j * T:(j + 1) * T, span(h)] = xg[j, :, span(h)].astype(F32)
        xb[:, span(h)] = xf[:, span(h)].astype(BF)
        rf[:, span(h)] = dot(select, xb[:, span(h)], NN)
        for j in range(NZ):
            s2[j, :, span(h)] = rf[2 * j:2 * j + 2, span(h)].astype(BF)
        exchange(s2, r2, p2_s, p2_r, out_peer, h)

    def block_of(member):
        return mod(y - z - member, NY)

    mine = block_of(m)
    right = at_x(mod(m + 1, NX))
    left = at_x(mod(m - 1, NX))
    far = NX // 2
    near = NX - 1 - far
    hops = [(far, near) if c % 2 == 0 else (near, far) for c in range(C)]
    per = C // H

    def cols(c):
        return pl.ds(c * CW, CW)

    def ag_copy(d, t, c):
        step = t if d == 0 else -t
        ref = ag.at[block_of(m - step), :, cols(c)]
        return rcopy(ref, ref, ag_s.at[d, t, c], ag_r.at[d, t, c], (right, left)[d])

    def ag_arrival(d, t, c):
        step = t + 1 if d == 0 else -(t + 1)
        ref = ag.at[block_of(m - step), :, cols(c)]
        rcopy(ref, ref, ag_s.at[d, t, c], ag_r.at[d, t, c], (right, left)[d]).wait_recv()

    for h in range(H):
        arrive(s2, r2, p2_s, p2_r, out_peer, h)
        for j in range(NZ):
            rg[2 * j:2 * j + 2, span(h)] = r2[j, :, span(h)].astype(F32)
        ag[mine, :, span(h)] = rg[:, span(h)].astype(BF)
        for c in range(h * per, (h + 1) * per):
            for d in range(2):
                if hops[c][d] > 0:
                    send(ag_copy(d, 0, c))

    loads[3].wait()
    loads[4].wait()
    loads[5].wait()
    dense_up = jnp.transpose(dot(dwd_v[...], xb[...], NT))
    dense_gg, dense_gu = swiglu_back(dense_up, dgp_v[...], dup_v[...])
    gg[y, 0] = dense_gg.astype(BF)
    gg[y, 1] = dense_gu.astype(BF)
    for k in range(1, NY):
        send(rcopy(gg.at[y], gg.at[y], gg_s.at[k], gg_r.at[k], at_yz(mod(y + k, NY), z)))

    def pass_on():
        for k in range(1, NZ):
            rcopy(
                wg.at[dp, z], wg.at[dp, mod(z - k, NZ)], wz_s.at[k], wz_r.at[k], at_yz(y, mod(z + k, NZ))
            ).wait_recv()
        send(rcopy(wg.at[dp], wg.at[dp], sib.at[0], sib.at[1], sibling))

    loads[6].wait()
    for t in range(1, far):
        for c in range(C):
            for d in range(2):
                if t < hops[c][d]:
                    ag_arrival(d, t - 1, c)
                    send(ag_copy(d, t, c))
        if t == 1:
            pass_on()
    if far == 1:
        pass_on()
    upstream = jnp.zeros((F, SL), F32)
    for c in range(C):
        for d in range(2):
            if hops[c][d] > 0:
                ag_arrival(d, hops[c][d] - 1, c)
        rows = ag[:, :, c * CW:(c + 1) * CW].reshape(SL, CW)
        upstream = upstream + dot(ewd_v[:, c * CW:(c + 1) * CW], rows, NT)
    loads[7].wait()
    loads[8].wait()
    expert_gg, expert_gu = [
        jnp.transpose(part).astype(BF) for part in swiglu_back(upstream, egp_v[...], eup_v[...])
    ]

    def rs_copy(d, t, c):
        goal = m + hops[c][0] - t if d == 0 else m - hops[c][1] + t
        src = bk.at[block_of(goal), :, cols(c)] if t == 0 else rs.at[d, t, :, cols(c)]
        return rcopy(src, rr.at[d, t, :, cols(c)], rs_s.at[d, t, c], rs_r.at[d, t, c], (right, left)[d])

    def rs_arrival(d, t, c):
        rcopy(
            bk.at[0, :, cols(c)], rr.at[d, t, :, cols(c)], rs_s.at[d, t, c], rs_r.at[d, t, c], (right, left)[d]
        ).wait_recv()

    loads[9].wait()
    loads[10].wait()
    for c in range(C):
        part = slice(c * CW, (c + 1) * CW)
        back = dot(expert_gg, ewg_v[:, part], NN) + dot(expert_gu, ewu_v[:, part], NN)
        bk[:, :, part] = back.astype(BF).reshape(NY, RB, CW)
        for d in range(2):
            if hops[c][d] > 0:
                send(rs_copy(d, 0, c))

    def rs_steps(t):
        for c in range(C):
            part = slice(c * CW, (c + 1) * CW)
            for d in range(2):
                if t < hops[c][d]:
                    rs_arrival(d, t - 1, c)
                    goal = m + hops[c][0] - t if d == 0 else m - hops[c][1] + t
                    both = rr[d, t - 1, :, part].astype(F32) + bk[block_of(goal), :, part].astype(F32)
                    rs[d, t, :, part] = both.astype(BF)
                    send(rs_copy(d, t, c))

    for k in range(1, NY):
        rcopy(
            gg.at[y], gg.at[mod(y - k, NY)], gg_s.at[k], gg_r.at[k], at_yz(mod(y + k, NY), z)
        ).wait_recv()
    rcopy(wg.at[1 - dp], wg.at[1 - dp], sib.at[0], sib.at[1], sibling).wait_recv()
    dense = jnp.zeros((NY * G, DB), F32)
    for which in range(2):
        for j in range(NZ):
            wf[which, j * DR:(j + 1) * DR, :] = wg[which, j].astype(F32)
        dense = dense + dot(gg[:, which].reshape(NY * G, F), wf[which].astype(BF), NT)
    do_s[...] = dense.astype(BF).reshape(NY, G, DB)
    for k in range(1, NY):
        goal = mod(y + k, NY)
        send(rcopy(do_s.at[goal], do_r.at[y], do_ss.at[k], do_rs.at[k], at_yz(goal, z)))
    do_r[y] = do_s[y]

    for t in range(1, far):
        rs_steps(t)
        if t == 1:
            flush()
    for k in range(1, NY):
        rcopy(
            do_s.at[y], do_r.at[mod(y - k, NY)], do_ss.at[k], do_rs.at[k], at_yz(mod(y + k, NY), z)
        ).wait_recv()
    pair = 2 if (2 * DB) % 128 == 0 and NY % 2 == 0 else NY
    for j in range(0, NY, pair):
        tot[:, j * DB:(j + pair) * DB] = jnp.concatenate(
            [do_r[j + i].astype(F32) for i in range(pair)], axis=1
        )

    for h in range(H):
        for c in range(h * per, (h + 1) * per):
            part = slice(c * CW, (c + 1) * CW)
            full = bk[mine, :, part].astype(F32)
            for d in range(2):
                if hops[c][d] > 0:
                    rs_arrival(d, hops[c][d] - 1, c)
                    full = full + rr[d, hops[c][d] - 1, :, part].astype(F32)
            rf[:, part] = full
        for j in range(NZ):
            s6[j, :, span(h)] = rf[2 * j:2 * j + 2, span(h)].astype(BF)
        exchange(s6, r6, p6_s, p6_r, in_peer, h)

    for h in range(H):
        arrive(s6, r6, p6_s, p6_r, in_peer, h)
        for j in range(NZ):
            rg[2 * j:2 * j + 2, span(h)] = r6[j, :, span(h)].astype(F32)
        tot[:, span(h)] = tot[:, span(h)] + dot(weights, rg[:, span(h)].astype(BF), TN)
        for j in range(NX):
            s8[j, :, span(h)] = tot[j * T:(j + 1) * T, span(h)].astype(BF)
        for k in order:
            goal = mod(m + k, NX)
            send(rcopy(
                s8.at[goal, :, half(h)], r8.at[m, :, half(h)], p8_s.at[h, k], p8_r.at[h, k], at_x(goal)
            ))
    flush()
    for first in firsts:

        @pl.when(other_pair)
        def _(first=first):
            first.wait_send()

    for h in range(H):
        total = xg[m, :, span(h)].astype(F32) + s8[m, :, span(h)].astype(F32)
        for k in order:
            source = mod(m - k, NX)
            rcopy(
                s8.at[0, :, half(h)], r8.at[source, :, half(h)], p8_s.at[h, k], p8_r.at[h, k], at_x(source)
            ).wait_recv()
        for j in range(1, NX):
            total = total + r8[mod(m + j, NX), :, span(h)].astype(F32)
        out[:, span(h)] = total.astype(BF)


def body(NX, NY, NZ, *args):
    grad, routes, probs, dgp, dup, dwg, dwu, dwd, egp, eup, ewg, ewu, ewd = args
    T, D = grad.shape
    G = NX * T
    F = dwd.shape[0]
    SL = egp.shape[1]
    routes, probs = routes.T, probs.T
    egp, eup, ewg, ewu = [jnp.swapaxes(part, 1, 2) for part in (egp, eup, ewg, ewu)]
    RB = SL // NY
    DR = dwg.shape[0]
    DB = DR * NZ
    C = 4
    far = NX // 2
    V = pltpu.VMEM
    dma = pltpu.SemaphoreType.DMA
    scratch = [
        V((NX, T, D), BF), V((G, D), F32), V((G, D), BF), V((2, G), jnp.int32), V((2, G), BF),
        V((G, F), BF), V((G, F), BF), V((F, D), BF), V((F, SL), BF), V((F, SL), BF),
        V((F, D), BF), V((F, D), BF), V((F, D), BF),
        V((2, NZ, DR, F), BF), V((2, DB, F), F32), V((NY, 2, G, F), BF),
        V((NY, G, DB), BF), V((NY, G, DB), BF), V((RB, D), F32), V((RB, D), F32),
        V((NZ, 2, D), BF), V((NZ, 2, D), BF), V((NZ, 2, D), BF), V((NZ, 2, D), BF),
        V((NY, RB, D), BF), V((NY, RB, D), BF),
        V((2, far, RB, D), BF), V((2, far, RB, D), BF),
        V((NX, T, D), BF), V((NX, T, D), BF), V((G, D), F32),
        dma((12,)), dma((2, NX)), dma((2, NX)), dma((NZ,)), dma((NZ,)), dma((2,)),
        dma((NY,)), dma((NY,)), dma((NY,)), dma((NY,)),
        dma((2, NZ)), dma((2, NZ)), dma((2, NZ)), dma((2, NZ)),
        dma((2, far, C)), dma((2, far, C)), dma((2, far, C)), dma((2, far, C)),
        dma((2, NX)), dma((2, NX)),
    ]
    flops = 2 * 3 * F * D * (SL + G)
    return pl.pallas_call(
        functools.partial(kernel, NX, NY, NZ, C),
        out_shape=jax.ShapeDtypeStruct((T, D), BF),
        in_specs=[pl.BlockSpec(memory_space=pl.ANY)] * 13,
        out_specs=pl.BlockSpec(memory_space=pltpu.VMEM),
        scratch_shapes=scratch,
        compiler_params=pltpu.CompilerParams(
            collective_id=0, has_side_effects=True, vmem_limit_bytes=62 * 1024 * 1024
        ),
        cost_estimate=pl.CostEstimate(
            flops=flops, bytes_accessed=8 * F * D, transcendentals=F * (SL + G)
        ),
        name="layer_back",
    )(grad, routes, probs, dgp, dup, dwg, dwu, dwd, egp, eup, ewg, ewu, ewd)


def solution(mesh):
    NX = mesh.shape["tensor"]
    NE = mesh.shape["expert"]
    NY = NX
    NZ = NE // NY
    return jax.shard_map(
        functools.partial(body, NX, NY, NZ),
        mesh=mesh,
        in_specs=(
            P(("dp", "expert", "tensor"), None),
            P(("dp", "expert"), None),
            P(("dp", "expert"), None),
            P(("dp", "expert"), "tensor"),
            P(("dp", "expert"), "tensor"),
            P("expert", "tensor"),
            P("expert", "tensor"),
            P("tensor", None),
            P(("dp", "expert"), None, "tensor"),
            P(("dp", "expert"), None, "tensor"),
            P("expert", None, "tensor"),
            P("expert", None, "tensor"),
            P("expert", "tensor", None),
        ),
        out_specs=P(("dp", "expert", "tensor"), None),
        check_vma=False,
    )
```

time: 88.6 us -> 85.7 us (0.967)
  Pallas kernels: 85.8 us -> 83.4 us
    pallas_call x1, Pallas kernels: 85.8 us -> 83.4 us  [body(): pl.pallas_call(functools.partial(kernel, NX, NY, NZ, C), out_shape=jax.Sh...]
where the time goes in v3:
time: 85.7 us; the launch traced here: 84.8 us
  Pallas kernels  83.4 us (97%)
  local copies, waits for them, and re-layouts  1.37 us (2%)
    pallas_call x1, Pallas kernels, body(): pl.pallas_call(functools.partial(kernel, NX, NY, NZ, C), out_shape=jax.Sh...  83.4 us

profile of v3, /device:TPU:14, one launch (start us, length us, event | category | flops | bytes accessed | tf_op | source)
XLA Modules:
  0.0 84.8 jit_solution(18011645162148002821)
XLA Ops:
  0.0 83.4 %layer_back.1 = bf16[4,3584]{1,0:T(4,128)(2,1)} custom-call(bf16[4,3584]{1,0:T(4,128)(2,1)} %grad.1, s32[2,32]{1,0:T(2,128)} %bitcast.10, bf16[2,32]{1,0:T(2,128)(2,1)} %bitcast.11, bf16[32,304]{1,0:T(8,128)(2,1)} %dgp.1, bf16[32,304]{1,0:T(8,128)(2,1)} %dup.1, bf16[56,304]{1,0:T(8,128)(2,1)} %dwg.1, bf16[56,304]{1,0:T(8,128)(2,1)} %dwu.1, ...), custom_call_target="tpu_custom_call" | custom-call | flops 1045954560 | bytes 8716288 | tf_op jit(solution)/shard_map/layer_back/pallas_call | solution.py:443
  83.4 1.4 %copy.15 = bf16[4,3584]{1,0:T(4,128)(2,1)} copy(bf16[4,3584]{1,0:T(4,128)(2,1)} %layer_back.1) | data formatting | bytes 57344

commit v4 on v3

v4 whole, which is shorter than its diff:
```python
import functools
import math

import jax
import jax.numpy as jnp
from jax import lax
from jax.experimental import pallas as pl
from jax.experimental.pallas import tpu as pltpu
from jax.sharding import PartitionSpec as P

BF = jnp.bfloat16
F32 = jnp.float32
NT = (((1,), (1,)), ((), ()))
TN = (((0,), (0,)), ((), ()))
NN = (((1,), (0,)), ((), ()))


def mod(value, n):
    return lax.rem(value + 4 * n, n)


def dot(a, b, dims):
    return lax.dot_general(a, b, dims, preferred_element_type=F32)


def swiglu_back(upstream, gate_pre, up_pre):
    gate = gate_pre.astype(F32)
    up = up_pre.astype(F32)
    sigma = 1.0 / (1.0 + jnp.exp(-gate))
    grad_gate = upstream * up * (sigma * (1.0 + gate * (1.0 - sigma)))
    grad_up = upstream * (gate * sigma)
    return grad_gate, grad_up


def kernel(
    NX, NY, NZ,
    grad, routes, probs, dgp, dup, dwg, dwu, dwd, egp, eup, ewg, ewu, ewd,
    out,
    xg, xf, xb, rt, pr, dgp_v, dup_v, dwd_v, egp_v, eup_v, ewd_v, ewg_v, ewu_v,
    wg, wf, gg, do_s, do_r, rf, rg, fs, s2, r2, s6, r6, ag, bk, r_one, r_two, s8, r8, tot,
    ld_sem, p1_s, p1_r, wz_s, wz_r, sib, gg_s, gg_r, do_ss, do_rs,
    p2_s, p2_r, p6_s, p6_r, ag_s, ag_r, rs_s, rs_r, p8_s, p8_r,
):
    T, D = grad.shape
    G = NX * T
    F = dwd.shape[0]
    RB = ag.shape[2]
    Q = NX // 2
    DB = do_s.shape[2]
    DR = dwg.shape[0]
    SL = NY * RB

    dp = lax.axis_index("dp")
    ex = lax.axis_index("expert")
    m = lax.axis_index("tensor")
    y = ex // NZ
    z = ex % NZ

    def rcopy(src, dst, ss, rsem, device):
        return pltpu.make_async_remote_copy(
            src_ref=src, dst_ref=dst, send_sem=ss, recv_sem=rsem,
            device_id=device, device_id_type=pl.DeviceIdType.MESH,
        )

    def at_x(x):
        return (dp, ex, x)

    def at_yz(yy, zz):
        return (dp, yy * NZ + zz, m)

    sibling = (1 - dp, ex, m)
    own_pair = [mod(m + i * Q + z, NY) == 0 for i in range(2)]
    other_pair = [jnp.logical_not(own) for own in own_pair]

    barrier = pltpu.get_barrier_semaphore()

    def greet(device):
        pl.semaphore_signal(barrier, inc=1, device_id=device, device_id_type=pl.DeviceIdType.MESH)

    def out_peer(i, k):
        zz = mod(z + k, NZ)
        return at_yz(mod(y + m + i * Q + zz, NY), zz)

    def in_peer(i, k):
        return at_yz(mod(y - m - i * Q - z, NY), mod(z + k, NZ))

    for k in range(1, NX):
        greet(at_x(mod(m + k, NX)))
    for i in range(2):
        for k in range(1, NZ):
            greet(in_peer(i, k))
            greet(out_peer(i, k))

        @pl.when(other_pair[i])
        def _(i=i):
            greet(in_peer(i, 0))
            greet(out_peer(i, 0))

    for k in range(1, NZ):
        greet(at_yz(y, mod(z + k, NZ)))
    for k in range(1, NY):
        greet(at_yz(mod(y + k, NY), z))
    greet(sibling)

    loads = [
        pltpu.make_async_copy(grad, xg.at[m], ld_sem.at[0]),
        pltpu.make_async_copy(routes, rt, ld_sem.at[1]),
        pltpu.make_async_copy(probs, pr, ld_sem.at[2]),
        pltpu.make_async_copy(dwd, dwd_v, ld_sem.at[3]),
        pltpu.make_async_copy(dgp, dgp_v, ld_sem.at[4]),
        pltpu.make_async_copy(dup, dup_v, ld_sem.at[5]),
        pltpu.make_async_copy(ewd.at[0], ewd_v, ld_sem.at[6]),
        pltpu.make_async_copy(egp.at[0], egp_v, ld_sem.at[7]),
        pltpu.make_async_copy(eup.at[0], eup_v, ld_sem.at[8]),
        pltpu.make_async_copy(ewg.at[0], ewg_v, ld_sem.at[9]),
        pltpu.make_async_copy(ewu.at[0], ewu_v, ld_sem.at[10]),
    ]
    own_gate = pltpu.make_async_copy(dwg, wg.at[0, z], ld_sem.at[11])
    own_up = pltpu.make_async_copy(dwu, wg.at[1, z], ld_sem.at[11])
    for load in loads[:3]:
        load.start()

    @pl.when(dp == 0)
    def _():
        own_gate.start()

    @pl.when(dp == 1)
    def _():
        own_up.start()

    for load in loads[3:]:
        load.start()

    fixed = NX - 1 + NY - 1 + NZ - 1 + 1 + 4 * (NZ - 1)
    others = other_pair[0].astype(jnp.int32) + other_pair[1].astype(jnp.int32)
    pl.semaphore_wait(barrier, fixed + 2 * others)

    sent = []

    def send(copy):
        copy.start()
        sent.append(copy)

    def flush():
        for copy in sent:
            copy.wait_send()
        sent.clear()

    H = 2
    HW = D // H

    def half(h):
        return pl.ds(h * HW, HW)

    def span(h):
        return slice(h * HW, (h + 1) * HW)

    order = sorted(range(1, NX), key=lambda k: -min(k, NX - k))

    def gather(h):
        for k in order:
            send(rcopy(
                grad.at[:, half(h)], xg.at[m, :, half(h)], p1_s.at[h, k], p1_r.at[h, k], at_x(mod(m + k, NX))
            ))

    gather(0)

    loads[1].wait()
    loads[2].wait()
    slot = lax.broadcasted_iota(jnp.int32, (2 * RB, G), 0)
    owner = (slot >= RB).astype(jnp.int32)
    zc = lax.shift_right_logical(slot - owner * RB, 1)
    named = jnp.bitwise_and(y + m + owner * Q + zc, NY - 1) * NZ + zc
    r0 = rt[0:1, :]
    r1 = rt[1:2, :]
    hit0 = (r0 == named).astype(F32)
    hit1 = (r1 == named).astype(F32)
    hits = hit0 + hit1
    earlier = (
        lax.broadcasted_iota(jnp.int32, (G, G), 0) < lax.broadcasted_iota(jnp.int32, (G, G), 1)
    ).astype(BF)
    rank = dot(hits.astype(BF), earlier, NN)
    taken = (rank == jnp.bitwise_and(slot, 1).astype(F32)).astype(F32)
    select = (hits * taken).astype(BF)
    pv = pr[...].astype(F32)
    weights = ((hit0 * pv[0:1, :] + hit1 * pv[1:2, :]) * taken).astype(BF)

    flush()
    gather(1)

    pltpu.make_async_copy(dwg, wg.at[0, z], ld_sem.at[11]).wait()
    for k in range(1, NZ):
        send(rcopy(wg.at[dp, z], wg.at[dp, z], wz_s.at[k], wz_r.at[k], at_yz(y, mod(z + k, NZ))))

    firsts = []

    def exchange(src, dst, ssem, rsem, peer, h):
        for i in range(2):
            local = pltpu.make_async_copy(src.at[i, z, :, half(h)], dst.at[i, z, :, half(h)], rsem.at[h, i, 0])

            @pl.when(own_pair[i])
            def _(local=local):
                local.start()

            first = rcopy(
                src.at[i, z, :, half(h)], dst.at[i, z, :, half(h)], ssem.at[h, i, 0], rsem.at[h, i, 0], peer(i, 0)
            )

            @pl.when(other_pair[i])
            def _(first=first):
                first.start()

            firsts.append((i, first))
            for k in range(1, NZ):
                send(rcopy(
                    src.at[i, mod(z + k, NZ), :, half(h)], dst.at[i, z, :, half(h)],
                    ssem.at[h, i, k], rsem.at[h, i, k], peer(i, k),
                ))

    def arrive(src, dst, ssem, rsem, peer, h):
        for i in range(2):
            for k in range(NZ):
                rcopy(
                    src.at[i, 0, :, half(h)], dst.at[i, mod(z - k, NZ), :, half(h)],
                    ssem.at[h, i, k], rsem.at[h, i, k], peer(i, k),
                ).wait_recv()

    def split_rows(rows, parts, h):
        for i in range(2):
            for j in range(NZ):
                low = i * RB + 2 * j
                parts[i, j, :, span(h)] = rows[low:low + 2, span(h)].astype(BF)

    def join_rows(rows, parts, h):
        for i in range(2):
            for j in range(NZ):
                low = i * RB + 2 * j
                rows[low:low + 2, span(h)] = parts[i, j, :, span(h)].astype(F32)

    loads[0].wait()
    for h in range(H):
        for k in order:
            source = mod(m - k, NX)
            rcopy(
                grad.at[:, half(h)], xg.at[source, :, half(h)], p1_s.at[h, k], p1_r.at[h, k], at_x(source)
            ).wait_recv()
        for j in range(NX):
            xf[j * T:(j + 1) * T, span(h)] = xg[j, :, span(h)].astype(F32)
        xb[:, span(h)] = xf[:, span(h)].astype(BF)
        rf[:, span(h)] = dot(select, xb[:, span(h)], NN)
        split_rows(rf, s2, h)
        exchange(s2, r2, p2_s, p2_r, out_peer, h)

    def block_of(member):
        return mod(y - z - member, NY)

    def slab(member):
        return block_of(member) % Q

    def side(member):
        return block_of(member) // Q

    loads[3].wait()
    loads[4].wait()
    loads[5].wait()
    dense_up = jnp.transpose(dot(dwd_v[...], xb[...], NT))
    dense_gg, dense_gu = swiglu_back(dense_up, dgp_v[...], dup_v[...])
    gg[y, 0] = dense_gg.astype(BF)
    gg[y, 1] = dense_gu.astype(BF)

    steps = [2, -2, 1, -1]

    def ag_copy(n, h, origin, goal):
        if n < 2:
            ref = ag.at[slab(origin), side(origin), :, half(h)]
        else:
            ref = ag.at[slab(origin), :, :, half(h)]
        return rcopy(ref, ref, ag_s.at[h, n], ag_r.at[h, n], at_x(mod(goal, NX)))

    for h in range(H):
        arrive(s2, r2, p2_s, p2_r, out_peer, h)
        join_rows(rg, r2, h)
        ag[slab(m), side(m), :, span(h)] = rg[0:RB, span(h)].astype(BF)
        ag[slab(m), 1 - side(m), :, span(h)] = rg[RB:2 * RB, span(h)].astype(BF)
        for n, step in enumerate(steps):
            send(ag_copy(n, h, m, m + step))

    for k in range(1, NY):
        send(rcopy(gg.at[y], gg.at[y], gg_s.at[k], gg_r.at[k], at_yz(mod(y + k, NY), z)))
    for k in range(1, NZ):
        rcopy(
            wg.at[dp, z], wg.at[dp, mod(z - k, NZ)], wz_s.at[k], wz_r.at[k], at_yz(y, mod(z + k, NZ))
        ).wait_recv()
    send(rcopy(wg.at[dp], wg.at[dp], sib.at[0], sib.at[1], sibling))

    loads[6].wait()
    upstream = jnp.zeros((F, SL), F32)
    for h in range(H):
        for n, step in enumerate(steps):
            ag_copy(n, h, m - step, m + step).wait_recv()
        rows = jnp.concatenate([ag[b % Q, b // Q, :, span(h)] for b in range(NY)], axis=0)
        upstream = upstream + dot(ewd_v[:, span(h)], rows, NT)
    loads[7].wait()
    loads[8].wait()
    expert_gg, expert_gu = [
        jnp.transpose(part).astype(BF) for part in swiglu_back(upstream, egp_v[...], eup_v[...])
    ]

    def rs_copy(n, h):
        goal = m + steps[n]
        if n < 2:
            src = bk.at[slab(goal), side(goal), :, half(h)]
            dst = r_two.at[n, :, half(h)]
        else:
            src = bk.at[slab(goal), :, :, half(h)]
            dst = r_one.at[n - 2, :, :, half(h)]
        return rcopy(src, dst, rs_s.at[h, n], rs_r.at[h, n], at_x(mod(goal, NX)))

    def back(h):
        rows = dot(expert_gg, ewg_v[:, span(h)], NN) + dot(expert_gu, ewu_v[:, span(h)], NN)
        rows = rows.astype(BF)
        for b in range(NY):
            bk[b % Q, b // Q, :, span(h)] = rows[b * RB:(b + 1) * RB]

    loads[9].wait()
    loads[10].wait()
    back(0)
    for n in range(4):
        send(rs_copy(n, 0))
    back(1)

    for k in range(1, NY):
        rcopy(
            gg.at[y], gg.at[mod(y - k, NY)], gg_s.at[k], gg_r.at[k], at_yz(mod(y + k, NY), z)
        ).wait_recv()
    rcopy(wg.at[1 - dp], wg.at[1 - dp], sib.at[0], sib.at[1], sibling).wait_recv()
    dense = jnp.zeros((NY * G, DB), F32)
    for which in range(2):
        for j in range(NZ):
            wf[which, j * DR:(j + 1) * DR, :] = wg[which, j].astype(F32)
        dense = dense + dot(gg[:, which].reshape(NY * G, F), wf[which].astype(BF), NT)
    do_s[...] = dense.astype(BF).reshape(NY, G, DB)
    for n in range(4):
        send(rs_copy(n, 1))
    for k in range(1, NY):
        goal = mod(y + k, NY)
        send(rcopy(do_s.at[goal], do_r.at[y], do_ss.at[k], do_rs.at[k], at_yz(goal, z)))
    do_r[y] = do_s[y]

    for h in range(H):
        for n in range(4):
            rs_copy(n, h).wait_recv()
        fs[:, :, span(h)] = (
            bk[slab(m), :, :, span(h)].astype(F32)
            + r_one[0, :, :, span(h)].astype(F32)
            + r_one[1, :, :, span(h)].astype(F32)
        )
        rf[0:RB, span(h)] = (
            fs[side(m), :, span(h)] + r_two[0, :, span(h)].astype(F32) + r_two[1, :, span(h)].astype(F32)
        )
        rf[RB:2 * RB, span(h)] = fs[1 - side(m), :, span(h)]
        split_rows(rf, s6, h)
        exchange(s6, r6, p6_s, p6_r, in_peer, h)

    for k in range(1, NY):
        rcopy(
            do_s.at[y], do_r.at[mod(y - k, NY)], do_ss.at[k], do_rs.at[k], at_yz(mod(y + k, NY), z)
        ).wait_recv()
    pair = 2 if (2 * DB) % 128 == 0 and NY % 2 == 0 else NY
    for j in range(0, NY, pair):
        tot[:, j * DB:(j + pair) * DB] = jnp.concatenate(
            [do_r[j + i].astype(F32) for i in range(pair)], axis=1
        )

    for h in range(H):
        arrive(s6, r6, p6_s, p6_r, in_peer, h)
        join_rows(rg, r6, h)
        tot[:, span(h)] = tot[:, span(h)] + dot(weights, rg[:, span(h)].astype(BF), TN)
        for j in range(NX):
            s8[j, :, span(h)] = tot[j * T:(j + 1) * T, span(h)].astype(BF)
        for k in order:
            goal = mod(m + k, NX)
            send(rcopy(
                s8.at[goal, :, half(h)], r8.at[m, :, half(h)], p8_s.at[h, k], p8_r.at[h, k], at_x(goal)
            ))
    flush()
    for i, first in firsts:

        @pl.when(other_pair[i])
        def _(first=first):
            first.wait_send()

    for h in range(H):
        total = xg[m, :, span(h)].astype(F32) + s8[m, :, span(h)].astype(F32)
        for k in order:
            source = mod(m - k, NX)
            rcopy(
                s8.at[0, :, half(h)], r8.at[source, :, half(h)], p8_s.at[h, k], p8_r.at[h, k], at_x(source)
            ).wait_recv()
        for j in range(1, NX):
            total = total + r8[mod(m + j, NX), :, span(h)].astype(F32)
        out[:, span(h)] = total.astype(BF)


def body(NX, NY, NZ, *args):
    grad, routes, probs, dgp, dup, dwg, dwu, dwd, egp, eup, ewg, ewu, ewd = args
    T, D = grad.shape
    G = NX * T
    F = dwd.shape[0]
    SL = egp.shape[1]
    routes, probs = routes.T, probs.T
    egp, eup, ewg, ewu = [jnp.swapaxes(part, 1, 2) for part in (egp, eup, ewg, ewu)]
    RB = SL // NY
    DR = dwg.shape[0]
    DB = DR * NZ
    Q = NX // 2
    V = pltpu.VMEM
    dma = pltpu.SemaphoreType.DMA
    scratch = [
        V((NX, T, D), BF), V((G, D), F32), V((G, D), BF), V((2, G), jnp.int32), V((2, G), BF),
        V((G, F), BF), V((G, F), BF), V((F, D), BF), V((F, SL), BF), V((F, SL), BF),
        V((F, D), BF), V((F, D), BF), V((F, D), BF),
        V((2, NZ, DR, F), BF), V((2, DB, F), F32), V((NY, 2, G, F), BF),
        V((NY, G, DB), BF), V((NY, G, DB), BF), V((2 * RB, D), F32), V((2 * RB, D), F32), V((2, RB, D), F32),
        V((2, NZ, 2, D), BF), V((2, NZ, 2, D), BF), V((2, NZ, 2, D), BF), V((2, NZ, 2, D), BF),
        V((Q, 2, RB, D), BF), V((Q, 2, RB, D), BF), V((2, 2, RB, D), BF), V((2, RB, D), BF),
        V((NX, T, D), BF), V((NX, T, D), BF), V((G, D), F32),
        dma((12,)), dma((2, NX)), dma((2, NX)), dma((NZ,)), dma((NZ,)), dma((2,)),
        dma((NY,)), dma((NY,)), dma((NY,)), dma((NY,)),
        dma((2, 2, NZ)), dma((2, 2, NZ)), dma((2, 2, NZ)), dma((2, 2, NZ)),
        dma((2, 4)), dma((2, 4)), dma((2, 4)), dma((2, 4)),
        dma((2, NX)), dma((2, NX)),
    ]
    flops = 2 * 3 * F * D * (SL + G)
    return pl.pallas_call(
        functools.partial(kernel, NX, NY, NZ),
        out_shape=jax.ShapeDtypeStruct((T, D), BF),
        in_specs=[pl.BlockSpec(memory_space=pl.ANY)] * 13,
        out_specs=pl.BlockSpec(memory_space=pltpu.VMEM),
        scratch_shapes=scratch,
        compiler_params=pltpu.CompilerParams(
            collective_id=0, has_side_effects=True, vmem_limit_bytes=62 * 1024 * 1024
        ),
        cost_estimate=pl.CostEstimate(
            flops=flops, bytes_accessed=8 * F * D, transcendentals=F * (SL + G)
        ),
        name="layer_back",
    )(grad, routes, probs, dgp, dup, dwg, dwu, dwd, egp, eup, ewg, ewu, ewd)


def solution(mesh):
    NX = mesh.shape["tensor"]
    NE = mesh.shape["expert"]
    NY = NX
    NZ = NE // NY
    return jax.shard_map(
        functools.partial(body, NX, NY, NZ),
        mesh=mesh,
        in_specs=(
            P(("dp", "expert", "tensor"), None),
            P(("dp", "expert"), None),
            P(("dp", "expert"), None),
            P(("dp", "expert"), "tensor"),
            P(("dp", "expert"), "tensor"),
            P("expert", "tensor"),
            P("expert", "tensor"),
            P("tensor", None),
            P(("dp", "expert"), None, "tensor"),
            P(("dp", "expert"), None, "tensor"),
            P("expert", None, "tensor"),
            P("expert", None, "tensor"),
            P("expert", "tensor", None),
        ),
        out_specs=P(("dp", "expert", "tensor"), None),
        check_vma=False,
    )
```

time: 85.7 us -> 78.3 us (0.914)
  Pallas kernels: 83.4 us -> 75.4 us
    pallas_call x1, Pallas kernels: 83.4 us -> 75.4 us  [body(): pl.pallas_call(functools.partial(kernel, NX, NY, NZ), out_shape=jax.Shape...]
where the time goes in v4:
time: 78.3 us; the launch traced here: 76.8 us
  Pallas kernels  75.4 us (96%)
  local copies, waits for them, and re-layouts  1.37 us (2%)
    pallas_call x1, Pallas kernels, body(): pl.pallas_call(functools.partial(kernel, NX, NY, NZ), out_shape=jax.Shape...  75.4 us

profile of v4, /device:TPU:14, one launch (start us, length us, event | category | flops | bytes accessed | tf_op | source)
XLA Modules:
  0.0 76.8 jit_solution(11034945583236436243)
XLA Ops:
  0.0 75.4 %layer_back.1 = bf16[4,3584]{1,0:T(4,128)(2,1)} custom-call(bf16[4,3584]{1,0:T(4,128)(2,1)} %grad.1, s32[2,32]{1,0:T(2,128)} %bitcast.10, bf16[2,32]{1,0:T(2,128)(2,1)} %bitcast.11, bf16[32,304]{1,0:T(8,128)(2,1)} %dgp.1, bf16[32,304]{1,0:T(8,128)(2,1)} %dup.1, bf16[56,304]{1,0:T(8,128)(2,1)} %dwg.1, bf16[56,304]{1,0:T(8,128)(2,1)} %dwu.1, ...), custom_call_target="tpu_custom_call" | custom-call | flops 1045954560 | bytes 8716288 | tf_op jit(solution)/shard_map/layer_back/pallas_call | solution.py:435
  75.4 1.4 %copy.15 = bf16[4,3584]{1,0:T(4,128)(2,1)} copy(bf16[4,3584]{1,0:T(4,128)(2,1)} %layer_back.1) | data formatting | bytes 57344

commit v5 on v4

--- a/solution.py
+++ b/solution.py
@@ -146,7 +146,7 @@
             copy.wait_send()
         sent.clear()
 
-    H = 2
+    H = HALVES
     HW = D // H
 
     def half(h):
@@ -163,7 +163,8 @@
                 grad.at[:, half(h)], xg.at[m, :, half(h)], p1_s.at[h, k], p1_r.at[h, k], at_x(mod(m + k, NX))
             ))
 
-    gather(0)
+    for h in range(H):
+        gather(h)
 
     loads[1].wait()
     loads[2].wait()
@@ -185,12 +186,6 @@
     pv = pr[...].astype(F32)
     weights = ((hit0 * pv[0:1, :] + hit1 * pv[1:2, :]) * taken).astype(BF)
 
-    flush()
-    gather(1)
-
-    pltpu.make_async_copy(dwg, wg.at[0, z], ld_sem.at[11]).wait()
-    for k in range(1, NZ):
-        send(rcopy(wg.at[dp, z], wg.at[dp, z], wz_s.at[k], wz_r.at[k], at_yz(y, mod(z + k, NZ))))
 
     firsts = []
 
@@ -211,7 +206,7 @@
                 first.start()
 
             firsts.append((i, first))
-            for k in range(1, NZ):
+            for k in sorted(range(1, NZ), key=lambda k: -min(k, NZ - k)):
                 send(rcopy(
                     src.at[i, mod(z + k, NZ), :, half(h)], dst.at[i, z, :, half(h)],
                     ssem.at[h, i, k], rsem.at[h, i, k], peer(i, k),
@@ -285,13 +280,11 @@
         for n, step in enumerate(steps):
             send(ag_copy(n, h, m, m + step))
 
+    pltpu.make_async_copy(dwg, wg.at[0, z], ld_sem.at[11]).wait()
+    for k in range(1, NZ):
+        send(rcopy(wg.at[dp, z], wg.at[dp, z], wz_s.at[k], wz_r.at[k], at_yz(y, mod(z + k, NZ))))
     for k in range(1, NY):
         send(rcopy(gg.at[y], gg.at[y], gg_s.at[k], gg_r.at[k], at_yz(mod(y + k, NY), z)))
-    for k in range(1, NZ):
-        rcopy(
-            wg.at[dp, z], wg.at[dp, mod(z - k, NZ)], wz_s.at[k], wz_r.at[k], at_yz(y, mod(z + k, NZ))
-        ).wait_recv()
-    send(rcopy(wg.at[dp], wg.at[dp], sib.at[0], sib.at[1], sibling))
 
     loads[6].wait()
     upstream = jnp.zeros((F, SL), F32)
@@ -324,10 +317,16 @@
 
     loads[9].wait()
     loads[10].wait()
-    back(0)
-    for n in range(4):
-        send(rs_copy(n, 0))
-    back(1)
+    for h in range(H):
+        back(h)
+        for n in range(4):
+            send(rs_copy(n, h))
+
+    for k in range(1, NZ):
+        rcopy(
+            wg.at[dp, z], wg.at[dp, mod(z - k, NZ)], wz_s.at[k], wz_r.at[k], at_yz(y, mod(z + k, NZ))
+        ).wait_recv()
+    send(rcopy(wg.at[dp], wg.at[dp], sib.at[0], sib.at[1], sibling))
 
     for k in range(1, NY):
         rcopy(
@@ -340,8 +339,6 @@
             wf[which, j * DR:(j + 1) * DR, :] = wg[which, j].astype(F32)
         dense = dense + dot(gg[:, which].reshape(NY * G, F), wf[which].astype(BF), NT)
     do_s[...] = dense.astype(BF).reshape(NY, G, DB)
-    for n in range(4):
-        send(rs_copy(n, 1))
     for k in range(1, NY):
         goal = mod(y + k, NY)
         send(rcopy(do_s.at[goal], do_r.at[y], do_ss.at[k], do_rs.at[k], at_yz(goal, z)))
@@ -400,6 +397,9 @@
         for j in range(1, NX):
             total = total + r8[mod(m + j, NX), :, span(h)].astype(F32)
         out[:, span(h)] = total.astype(BF)
+
+
+HALVES = 2
 
 
 def body(NX, NY, NZ, *args):
@@ -425,11 +425,11 @@
         V((2, NZ, 2, D), BF), V((2, NZ, 2, D), BF), V((2, NZ, 2, D), BF), V((2, NZ, 2, D), BF),
         V((Q, 2, RB, D), BF), V((Q, 2, RB, D), BF), V((2, 2, RB, D), BF), V((2, RB, D), BF),
         V((NX, T, D), BF), V((NX, T, D), BF), V((G, D), F32),
-        dma((12,)), dma((2, NX)), dma((2, NX)), dma((NZ,)), dma((NZ,)), dma((2,)),
+        dma((12,)), dma((HALVES, NX)), dma((HALVES, NX)), dma((NZ,)), dma((NZ,)), dma((2,)),
         dma((NY,)), dma((NY,)), dma((NY,)), dma((NY,)),
-        dma((2, 2, NZ)), dma((2, 2, NZ)), dma((2, 2, NZ)), dma((2, 2, NZ)),
-        dma((2, 4)), dma((2, 4)), dma((2, 4)), dma((2, 4)),
-        dma((2, NX)), dma((2, NX)),
+        dma((HALVES, 2, NZ)), dma((HALVES, 2, NZ)), dma((HALVES, 2, NZ)), dma((HALVES, 2, NZ)),
+        dma((HALVES, 4)), dma((HALVES, 4)), dma((HALVES, 4)), dma((HALVES, 4)),
+        dma((HALVES, NX)), dma((HALVES, NX)),
     ]
     flops = 2 * 3 * F * D * (SL + G)
     return pl.pallas_call(

time: 78.3 us -> 79.4 us (1.014)
  Pallas kernels: 75.4 us -> 77 us
    pallas_call x1, Pallas kernels: 75.4 us -> 77 us  [body(): pl.pallas_call(functools.partial(kernel, NX, NY, NZ), out_shape=jax.Shape...]
where the time goes in v5:
time: 79.4 us; the launch traced here: 78.4 us
  Pallas kernels  77 us (97%)
  local copies, waits for them, and re-layouts  1.37 us (2%)
    pallas_call x1, Pallas kernels, body(): pl.pallas_call(functools.partial(kernel, NX, NY, NZ), out_shape=jax.Shape...  77 us

profile of v5, /device:TPU:14, one launch (start us, length us, event | category | flops | bytes accessed | tf_op | source)
XLA Modules:
  0.0 78.4 jit_solution(8743850755269059988)
XLA Ops:
  0.0 77.0 %layer_back.1 = bf16[4,3584]{1,0:T(4,128)(2,1)} custom-call(bf16[4,3584]{1,0:T(4,128)(2,1)} %grad.1, s32[2,32]{1,0:T(2,128)} %bitcast.10, bf16[2,32]{1,0:T(2,128)(2,1)} %bitcast.11, bf16[32,304]{1,0:T(8,128)(2,1)} %dgp.1, bf16[32,304]{1,0:T(8,128)(2,1)} %dup.1, bf16[56,304]{1,0:T(8,128)(2,1)} %dwg.1, bf16[56,304]{1,0:T(8,128)(2,1)} %dwu.1, ...), custom_call_target="tpu_custom_call" | custom-call | flops 1045954560 | bytes 8716288 | tf_op jit(solution)/shard_map/layer_back/pallas_call | solution.py:435
  77.0 1.4 %copy.15 = bf16[4,3584]{1,0:T(4,128)(2,1)} copy(bf16[4,3584]{1,0:T(4,128)(2,1)} %layer_back.1) | data formatting | bytes 57344
